TPU v7x, 32 devices: a whole 2x2x4 slice. The times are simulated.
32 devices in a mesh: section: 2 (over x), dp: 16 (over z, y, core).
Axes of the slice: x: 2, y: 2, z: 4, core: 2. Of those that a mesh axis runs over, the one named last changes fastest.
Arguments:
- center_data: bfloat16 [2, 384, 300], P('section', 'dp'), may hold values from -6 to 6
- edge_data: bfloat16 [2, 384, 100, 300], P('section', 'dp'), may hold values from -6 to 6
- leaf_counts: int32 [384], P('dp'), may hold values from 10 to 100, as said below
- leaf_mask: int32 [384, 100], P('dp'), may hold values 0 or 1
- square_weights: bfloat16 [2, 4, 300, 300], P('section'), may hold values from -0.375 to 0.375
- out_weight: bfloat16 [2, 300, 300], P('section'), may hold values from -1.5 to 1.5
- up_weight: bfloat16 [2, 300, 1200], P('section'), may hold values from -0.375 to 0.375
- down_weight: bfloat16 [2, 1200, 300], P('section'), may hold values from -0.1875 to 0.1875
- norm_gains: bfloat16 [2, 3, 300], P('section'), may hold values from 0.5 to 1.5
- biases: bfloat16 [2, 8, 300], P('section'), may hold values from -1.5 to 1.5
- hidden_bias: bfloat16 [2, 1200], P('section'), may hold values from -1.5 to 1.5
Outputs:
- center_result: bfloat16 [2, 384, 300], P('section', 'dp')
- edge_result: bfloat16 [2, 384, 100, 300], P('section', 'dp')
- grad_square: float32 [2, 4, 300, 300], P('section')
- grad_out_weight: float32 [2, 300, 300], P('section')
- grad_up: float32 [2, 300, 1200], P('section')
- grad_down: float32 [2, 1200, 300], P('section')
- grad_norm_gains: float32 [2, 3, 300], P('section')
- grad_biases: float32 [2, 8, 300], P('section')
- grad_hidden_bias: float32 [2, 1200], P('section')
- norms: float32 [2, 5, 384], P('section', None, 'dp')
Inputs may be any that keep to these rules, and one draw needn't show every extreme that they name: The first leaf_counts[g] leaf slots of star g may hold leaves; both ends occur in every draw.
All inputs are finite; a program needn't handle non-finite values. No bound on the sum of `leaf_mask` on one device may be relied on, other than what follows from the above.
Results may differ from a plain program's by a relative error of at most 0.015.
Values may be sent and summed in bfloat16 or wider, within the bound.
A program may use at most 192 MiB of HBM per device.

v0:
```python
import jax
import jax.numpy as jnp
from jax import lax
from jax.sharding import PartitionSpec as P

HEADS = 12
MICRO = 6


EPSILON = 1e-05
MASKED_SCORE = -1e30


def passed_along(block, axis, distance):
    devices = range(lax.axis_size(axis))
    route = [(i - distance, i) for i in devices if i - distance in devices]
    return lax.ppermute(block, axis, route)


def layer_norm(values, gain_row, bias_row):
    centred = values - jnp.mean(values, axis=-1, keepdims=True)
    spread = jnp.mean(centred * centred, axis=-1, keepdims=True)
    return centred * lax.rsqrt(spread + EPSILON) * gain_row + bias_row


def gelu_exact(values):
    return jax.nn.gelu(values, approximate=False)


def product(operand, factor):
    return jnp.dot(operand, factor, preferred_element_type=jnp.float32)


def against(operand, factor):
    return jnp.einsum("na,ba->nb", operand, factor, preferred_element_type=jnp.float32)


def outer_sum(operand, factor):
    return jnp.einsum("na,nb->ab", operand, factor, preferred_element_type=jnp.float32)


def total_rows(values):
    return jnp.sum(values.astype(jnp.float32), axis=0)


def root_square(values, axes):
    return jnp.sqrt(jnp.mean(values * values, axis=axes))


def zero_like(layer_tree):
    return jax.tree.map(lambda weight_leaf: jnp.zeros(weight_leaf.shape, jnp.float32), layer_tree)


def accumulate(running, fresh, scale_by):
    return jax.tree.map(lambda held_sum, extra_sum: held_sum + scale_by * extra_sum, running, fresh)


def forward_layer(layer_tree, centre, edges, live_slots):
    square, out_matrix, up_matrix, down_matrix, gain_rows, bias_rows, hidden_shift = layer_tree
    gain_rows = gain_rows.astype(jnp.float32)
    bias_rows = bias_rows.astype(jnp.float32)
    hidden_shift = hidden_shift.astype(jnp.float32)
    star_count, slot_count, model_width = edges.shape
    head_size = model_width // HEADS
    scaling = head_size ** (-0.5)
    centre_norm = layer_norm(centre, gain_rows[0], bias_rows[0]).astype(jnp.bfloat16)
    edge_norm = layer_norm(edges, gain_rows[1], bias_rows[1]).astype(jnp.bfloat16)
    edge_flat = edge_norm.reshape(star_count * slot_count, model_width)
    query = (product(centre_norm, square[0]) + bias_rows[3]).astype(jnp.bfloat16)
    key_rows = jnp.concatenate(
        [
            product(centre_norm, square[1])[:, None],
            product(edge_flat, square[1]).reshape(star_count, slot_count, model_width),
        ],
        1,
    ).astype(jnp.bfloat16)
    value_rows = (
        jnp.concatenate(
            [
                product(centre_norm, square[2])[:, None],
                product(edge_flat, square[2]).reshape(star_count, slot_count, model_width),
            ],
            1,
        )
        + bias_rows[4]
    ).astype(jnp.bfloat16)
    query_heads = query.reshape(star_count, HEADS, head_size)
    key_heads = key_rows.reshape(star_count, slot_count + 1, HEADS, head_size)
    value_heads = value_rows.reshape(star_count, slot_count + 1, HEADS, head_size)
    scores = (
        jnp.einsum("bhd,blhd->bhl", query_heads, key_heads, preferred_element_type=jnp.float32)
        * scaling
    )
    allowed = (
        jnp.concatenate([jnp.ones((star_count, 1), jnp.float32), live_slots], 1)[:, None, :] > 0
    )
    prob_rows = jax.nn.softmax(jnp.where(allowed, scores, MASKED_SCORE), axis=-1)
    prob_low = prob_rows.astype(jnp.bfloat16)
    attended = (
        jnp.einsum("bhl,blhd->bhd", prob_low, value_heads, preferred_element_type=jnp.float32)
        .reshape(star_count, model_width)
        .astype(jnp.bfloat16)
    )
    branch_attn = product(attended, out_matrix) + bias_rows[5]
    middle = centre + branch_attn
    gate_in = (edge_norm.astype(jnp.float32) * centre_norm.astype(jnp.float32)[:, None, :]).astype(
        jnp.bfloat16
    )
    gate_flat = gate_in.reshape(star_count * slot_count, model_width)
    branch_edge = (product(gate_flat, square[3]) + bias_rows[6]).reshape(
        star_count, slot_count, model_width
    )
    update = live_slots[:, :, None] * branch_edge
    edges_out = edges + update
    feed_norm = layer_norm(middle, gain_rows[2], bias_rows[2]).astype(jnp.bfloat16)
    hidden = product(feed_norm, up_matrix) + hidden_shift
    active = gelu_exact(hidden).astype(jnp.bfloat16)
    branch_ffn = product(active, down_matrix) + bias_rows[7]
    centre_out = middle + branch_ffn
    norm_rows = jnp.stack(
        [
            root_square(centre_out, -1),
            root_square(edges_out, (1, 2)),
            root_square(branch_attn, -1),
            root_square(update, (1, 2)),
            root_square(branch_ffn, -1),
        ]
    )
    saved = (
        centre_norm,
        edge_flat,
        query_heads,
        key_heads,
        value_heads,
        prob_rows,
        prob_low,
        attended,
        middle,
        gate_flat,
        feed_norm,
        hidden,
        active,
    )
    return (centre_out, edges_out, norm_rows, saved)


def backward_layer(layer_tree, centre, edges, live_slots, saved, grad_centre, grad_edges):
    square, out_matrix, up_matrix, down_matrix, gain_rows, bias_rows, hidden_shift = layer_tree
    gain_rows = gain_rows.astype(jnp.float32)
    bias_rows = bias_rows.astype(jnp.float32)
    (
        centre_norm,
        edge_flat,
        query_heads,
        key_heads,
        value_heads,
        prob_rows,
        prob_low,
        attended,
        middle,
        gate_flat,
        feed_norm,
        hidden,
        active,
    ) = saved
    star_count, slot_count, model_width = edges.shape
    head_size = model_width // HEADS
    scaling = head_size ** (-0.5)
    grad_ffn = grad_centre.astype(jnp.bfloat16)
    grad_down = outer_sum(active, grad_ffn)
    grad_active = against(grad_ffn, down_matrix)
    grad_hidden = jax.vjp(gelu_exact, hidden)[1](grad_active)[0].astype(jnp.bfloat16)
    grad_up = outer_sum(feed_norm, grad_hidden)
    grad_feed = against(grad_hidden, up_matrix)
    feed_back = jax.vjp(layer_norm, middle, gain_rows[2], bias_rows[2])[1]
    middle_part, gain_feed, bias_feed = feed_back(grad_feed)
    grad_middle = grad_centre + middle_part
    grad_update = (
        (live_slots[:, :, None] * grad_edges)
        .astype(jnp.bfloat16)
        .reshape(star_count * slot_count, model_width)
    )
    grad_gate_weight = outer_sum(gate_flat, grad_update)
    grad_gate = (
        against(grad_update, square[3])
        .astype(jnp.bfloat16)
        .astype(jnp.float32)
        .reshape(star_count, slot_count, model_width)
    )
    edge_norm = edge_flat.astype(jnp.float32).reshape(star_count, slot_count, model_width)
    grad_edge_norm = grad_gate * centre_norm.astype(jnp.float32)[:, None, :]
    grad_centre_norm = jnp.sum(grad_gate * edge_norm, axis=1)
    grad_attn = grad_middle.astype(jnp.bfloat16)
    grad_out = outer_sum(attended, grad_attn)
    grad_attended = (
        against(grad_attn, out_matrix).astype(jnp.bfloat16).reshape(star_count, HEADS, head_size)
    )
    grad_values = (
        jnp.einsum("bhl,bhd->blhd", prob_low, grad_attended, preferred_element_type=jnp.float32)
        .astype(jnp.bfloat16)
        .reshape(star_count, slot_count + 1, model_width)
    )
    grad_probs = jnp.einsum(
        "bhd,blhd->bhl", grad_attended, value_heads, preferred_element_type=jnp.float32
    )
    grad_scores = (
        prob_rows * (grad_probs - jnp.sum(prob_rows * grad_probs, axis=-1, keepdims=True))
    ).astype(jnp.bfloat16)
    grad_query = (
        (
            jnp.einsum("bhl,blhd->bhd", grad_scores, key_heads, preferred_element_type=jnp.float32)
            * scaling
        )
        .astype(jnp.bfloat16)
        .reshape(star_count, model_width)
    )
    grad_keys = (
        (
            jnp.einsum(
                "bhl,bhd->blhd", grad_scores, query_heads, preferred_element_type=jnp.float32
            )
            * scaling
        )
        .astype(jnp.bfloat16)
        .reshape(star_count, slot_count + 1, model_width)
    )
    key_centre = grad_keys[:, 0]
    key_leaves = grad_keys[:, 1:].reshape(star_count * slot_count, model_width)
    value_centre = grad_values[:, 0]
    value_leaves = grad_values[:, 1:].reshape(star_count * slot_count, model_width)
    grad_query_weight = outer_sum(centre_norm, grad_query)
    grad_key_weight = outer_sum(centre_norm, key_centre) + outer_sum(edge_flat, key_leaves)
    grad_value_weight = outer_sum(centre_norm, value_centre) + outer_sum(edge_flat, value_leaves)
    grad_centre_norm = (
        grad_centre_norm
        + against(grad_query, square[0])
        + against(key_centre, square[1])
        + against(value_centre, square[2])
    )
    grad_edge_norm = grad_edge_norm + (
        against(key_leaves, square[1]) + against(value_leaves, square[2])
    ).reshape(star_count, slot_count, model_width)
    centre_back = jax.vjp(layer_norm, centre, gain_rows[0], bias_rows[0])[1]
    centre_part, gain_centre, bias_centre = centre_back(grad_centre_norm)
    edge_back = jax.vjp(layer_norm, edges, gain_rows[1], bias_rows[1])[1]
    edge_part, gain_edge, bias_edge = edge_back(grad_edge_norm)
    gradients = (
        jnp.stack([grad_query_weight, grad_key_weight, grad_value_weight, grad_gate_weight]),
        grad_out,
        grad_up,
        grad_down,
        jnp.stack([gain_centre, gain_edge, gain_feed]),
        jnp.stack(
            [
                bias_centre,
                bias_edge,
                bias_feed,
                total_rows(grad_query),
                total_rows(value_centre) + total_rows(value_leaves),
                total_rows(grad_attn),
                total_rows(grad_update),
                total_rows(grad_ffn),
            ]
        ),
        total_rows(grad_hidden),
    )
    return (grad_middle + centre_part, grad_edges + edge_part, gradients)


def on_device(
    center_data,
    edge_data,
    leaf_counts,
    leaf_mask,
    square_weights,
    out_weight,
    up_weight,
    down_weight,
    norm_gains,
    biases,
    hidden_bias,
):
    star_count = center_data.shape[1]
    model_width = center_data.shape[2]
    slot_count = edge_data.shape[2]
    block_size = star_count // MICRO
    slot_index = lax.broadcasted_iota(jnp.int32, (star_count, slot_count), 1)
    live_slots = ((slot_index < leaf_counts[:, None]) & (leaf_mask > 0)).astype(jnp.float32)
    own_layer = (
        square_weights[0],
        out_weight[0],
        up_weight[0],
        down_weight[0],
        norm_gains[0],
        biases[0],
        hidden_bias[0],
    )
    own_centre = center_data[0]
    own_edges = edge_data[0]
    section_at = lax.axis_index("section")
    is_first = section_at == 0
    zero_centre = jnp.zeros((block_size, model_width), jnp.bfloat16)
    zero_edges = jnp.zeros((block_size, slot_count, model_width), jnp.bfloat16)
    got_centre, got_edges = (zero_centre, zero_edges)
    stored = []
    finished = []
    for tick_index in range(MICRO + 1):
        start_row = jnp.clip(tick_index - section_at, 0, MICRO - 1) * block_size
        mine_centre = lax.dynamic_slice_in_dim(own_centre, start_row, block_size, 0)
        mine_edges = lax.dynamic_slice_in_dim(own_edges, start_row, block_size, 0)
        take_centre = jnp.where(is_first, mine_centre, got_centre)
        take_edges = jnp.where(is_first, mine_edges, got_edges)
        piece_live = lax.dynamic_slice_in_dim(live_slots, start_row, block_size, 0)
        centre_out, edges_out, norm_rows, unused = forward_layer(
            own_layer, take_centre.astype(jnp.float32), take_edges.astype(jnp.float32), piece_live
        )
        sent_centre = centre_out.astype(jnp.bfloat16)
        sent_edges = edges_out.astype(jnp.bfloat16)
        stored.append((take_centre, take_edges))
        finished.append((sent_centre, sent_edges, norm_rows))
        if tick_index < MICRO:
            got_centre, got_edges = passed_along((sent_centre, sent_edges), "section", 1)
    back_centre, back_edges = (zero_centre, zero_edges)
    partial_value = zero_like(own_layer)
    returned = []
    for tick_index in range(MICRO + 1):
        batch_at = tick_index - 1 + section_at
        valid = ((batch_at >= 0) & (batch_at < MICRO)).astype(jnp.float32)
        start_row = jnp.clip(batch_at, 0, MICRO - 1) * block_size
        lower_saved = stored[max(tick_index - 1, 0)]
        upper_saved = stored[min(tick_index + 1, MICRO)]
        centre_in = jnp.where(is_first, lower_saved[0], upper_saved[0]).astype(jnp.float32)
        edges_in = jnp.where(is_first, lower_saved[1], upper_saved[1]).astype(jnp.float32)
        cot_centre = jnp.where(
            is_first, back_centre, lax.dynamic_slice_in_dim(own_centre, start_row, block_size, 0)
        )
        cot_edges = jnp.where(
            is_first, back_edges, lax.dynamic_slice_in_dim(own_edges, start_row, block_size, 0)
        )
        piece_live = lax.dynamic_slice_in_dim(live_slots, start_row, block_size, 0)
        unused_centre, unused_edges, unused_norms, saved = forward_layer(
            own_layer, centre_in, edges_in, piece_live
        )
        grad_centre, grad_edges, fresh = backward_layer(
            own_layer,
            centre_in,
            edges_in,
            piece_live,
            saved,
            cot_centre.astype(jnp.float32),
            cot_edges.astype(jnp.float32),
        )
        partial_value = accumulate(partial_value, fresh, valid)
        sent_centre = grad_centre.astype(jnp.bfloat16)
        sent_edges = grad_edges.astype(jnp.bfloat16)
        returned.append((sent_centre, sent_edges))
        if tick_index < MICRO:
            back_centre, back_edges = passed_along((sent_centre, sent_edges), "section", -1)
    centre_result = jnp.concatenate(
        [
            jnp.where(is_first, returned[micro_at + 1][0], finished[micro_at + 1][0])
            for micro_at in range(MICRO)
        ],
        0,
    )
    edge_result = jnp.concatenate(
        [
            jnp.where(is_first, returned[micro_at + 1][1], finished[micro_at + 1][1])
            for micro_at in range(MICRO)
        ],
        0,
    )
    norm_result = jnp.concatenate(
        [
            jnp.where(is_first, finished[micro_at][2], finished[micro_at + 1][2])
            for micro_at in range(MICRO)
        ],
        1,
    )
    summed = lax.psum(
        (
            partial_value[0],
            partial_value[1],
            partial_value[2],
            partial_value[3],
            partial_value[4],
            partial_value[5],
            partial_value[6],
        ),
        "dp",
    )
    return (
        centre_result[None],
        edge_result[None],
        summed[0][None],
        summed[1][None],
        summed[2][None],
        summed[3][None],
        summed[4][None],
        summed[5][None],
        summed[6][None],
        norm_result[None],
    )


def solution(mesh):
    return jax.shard_map(
        on_device,
        mesh=mesh,
        in_specs=(
            P("section", "dp", None),
            P("section", "dp", None, None),
            P("dp"),
            P("dp", None),
            P("section", None, None, None),
            P("section", None, None),
            P("section", None, None),
            P("section", None, None),
            P("section", None, None),
            P("section", None, None),
            P("section", None),
        ),
        out_specs=(
            P("section", "dp", None),
            P("section", "dp", None, None),
            P("section", None, None, None),
            P("section", None, None),
            P("section", None, None),
            P("section", None, None),
            P("section", None, None),
            P("section", None, None),
            P("section", None),
            P("section", None, "dp"),
        ),
        check_vma=False,
    )
```

profile of v0, /device:TPU:0, one launch (start us, length us, event | category | flops | bytes accessed | tf_op | source)
XLA Modules:
  0.0 1116.7 jit_solution(2843191020069204727)
XLA Ops:
  7.3 5.1 fusion.1778
  15.2 7.6 constant_dynamic-slice_fusion.1
  37.2 3.0 multiply_reduce_fusion.32
  40.2 5.7 collective-permute-start
  75.5 2.8 multiply_reduce_fusion.13
  110.0 3.1 multiply_reduce_fusion.29
  152.5 3.1 multiply_reduce_fusion.26
  216.6 2.5 convolution_bitcast_fusion.18
  230.6 3.0 multiply_reduce_fusion.23
  261.4 2.5 convolution_bitcast_fusion.20
  263.9 2.4 convolution_bitcast_fusion.19
  270.6 2.8 fusion.367
  275.8 2.8 multiply_reduce_fusion.10
  280.5 2.6 multiply_reduce_fusion.3
  283.1 2.5 collective-permute-start.12
  319.3 2.2 convolution_convert_fusion.5
  330.9 2.6 multiply_reduce_fusion.2
  349.1 3.1 multiply_reduce_fusion.20
  367.1 2.2 fusion.368
  429.1 2.4 convolution_bitcast_fusion.17
  431.4 2.3 convolution_bitcast_fusion.16
  447.6 3.0 fusion.37
  450.6 2.3 fusion.43
  460.5 2.4 convert_reduce_fusion.19
  468.8 3.4 add_reduce_fusion.5
  474.2 2.4 convolution_bitcast_fusion.15
  480.8 2.8 multiply_reduce_fusion.8
  485.5 2.6 multiply_reduce_fusion.1
  488.2 6.4 collective-permute-start.20
  502.9 3.1 multiply_reduce_fusion.17
  526.4 2.5 select_dynamic-update-slice_fusion.4
  611.7 3.0 multiply_reduce_fusion.14
  622.8 2.8 multiply_reduce_fusion.7
  627.6 2.6 convert_reduce_fusion.7
  645.9 5.5 fusion.238
  668.8 2.3 convolution_bitcast_fusion.14
  671.1 2.3 convolution_bitcast_fusion.13
  704.1 2.8 add_reduce_fusion.4
  709.0 2.4 convolution_bitcast_fusion.12
  719.8 2.5 select_dynamic-update-slice_fusion.3
  751.2 2.3 convolution_bitcast_fusion.11
  753.5 2.3 convolution_bitcast_fusion.10
  776.9 2.8 add_reduce_fusion.3
  788.0 2.2 select_dynamic-update-slice_fusion.2
  810.3 2.3 convolution_bitcast_fusion.8
  812.7 2.3 convolution_bitcast_fusion.7
  836.1 2.8 add_reduce_fusion.2
  847.2 2.3 select_dynamic-update-slice_fusion.1
  869.0 2.3 convolution_bitcast_fusion.5
  871.3 2.3 convolution_bitcast_fusion.4
  893.9 2.8 add_reduce_fusion.1
  904.8 2.2 select_dynamic-update-slice_fusion
  923.0 2.3 convolution_bitcast_fusion.2
  925.4 2.3 convolution_bitcast_fusion.1
  935.1 3.2 fusion.48
  945.9 3.4 fusion.47
  961.3 5.9 fusion.55
  969.1 2.2 fusion.445
  971.6 3.0 copy.813
  976.9 62.6 %all-reduce.14 = (f32[1,3,300]{2,0,1:T(1,128)}, f32[1,8,300]{2,1,0:T(8,128)}, f32[1,1200]{1,0:T(1,128)}) all-reduce(f32[1,3,300]{2,0,1:T(1,128)S(1)} %broadcast_in_dim.263, f32[1,8,300]{2,1,0:T(8,128)S(1)} %add_bitcast_fusion, f32[1,1200]{1,0:T(1,128)S(1)} %copy-done.340), channel_id=1, replica_groups=mesh['section'=2,'dp'=16] {'dp'}, use_global_device_ids=true, to_apply=%region_193.194 | all-reduce | flops 4500 | bytes 36000 | tf_op jit(solution)/shard_map/psum | solution.py:380
  1039.5 59.9 %all-reduce.18.cloned.1.call-done = (f32[1,4,300,300]{3,2,1,0:T(8,128)}, f32[1,300,300]{2,1,0:T(8,128)}, f32[1,300,1200]{2,1,0:T(8,128)}, f32[1,1200,300]{1,2,0:T(8,128)}) async-done(((f32[1,4,300,300]{3,2,1,0:T(8,128)}, f32[1,300,300]{2,1,0:T(8,128)}, f32[1,300,1200]{2,1,0:T(8,128)}, f32[1,1200,300]{1,2,0:T(8,128)}), (f32[1,4,300,300]{3,2,1,0:T(8,128)}, f32[1,300,300]{2,1,0:T(8,128)}, ...) | async-done | bytes 4680016 | tf_op jit(solution)/shard_map/psum | solution.py:380
  1099.4 3.6 copy.814
  1103.0 2.7 copy.816
  1105.7 2.7 copy.817
  (2106 shorter events, 789.7 us)
Async XLA Ops:
  7.2 30.0 %copy-start = (bf16[1,300,1200]{2,1,0:T(8,128)(2,1)S(1)}, bf16[1,300,1200]{2,1,0:T(8,128)(2,1)}, u32[]{:S(2)}) copy-start(bf16[1,300,1200]{2,1,0:T(8,128)(2,1)} %param.17) | copy-start | bytes 2160004
  7.2 1092.2 %all-reduce.18.cloned.1.call-start = ((), (), s32[]{:S(2)}) async-start(), calls=%async_computation | async-start | bytes 10895360 | tf_op jit(solution)/shard_map/psum | solution.py:380
  22.8 25.5 %copy-start.56 = (bf16[1,4,100,300]{3,1,2,0:T(4,128)(2,1)}, bf16[1,4,100,300]{3,1,2,0:T(4,128)(2,1)S(1)}, u32[]{:S(2)}) copy-start(bf16[1,4,100,300]{3,1,2,0:T(4,128)(2,1)S(1)} %get-tuple-element.366) | copy-start | bytes 720004
  24.0 323.7 %copy-start.138 = (f32[300]{0:T(512)}, f32[300]{0:T(512)S(1)}, u32[]{:S(2)}) copy-start(f32[300]{0:T(512)S(1)} %get-tuple-element.596) | copy-start | bytes 3604
  24.0 325.1 %copy-start.135 = (f32[300]{0:T(512)}, f32[300]{0:T(512)S(1)}, u32[]{:S(2)}) copy-start(f32[300]{0:T(512)S(1)} %get-tuple-element.593) | copy-start | bytes 3604
  24.0 352.5 %copy-start.141 = (f32[300]{0:T(512)}, f32[300]{0:T(512)S(1)}, u32[]{:S(2)}) copy-start(f32[300]{0:T(512)S(1)} %get-tuple-element.154) | copy-start | bytes 3604
  24.0 352.5 %copy-start.169 = (f32[300]{0:T(512)}, f32[300]{0:T(512)S(1)}, u32[]{:S(2)}) copy-start(f32[300]{0:T(512)S(1)} %get-tuple-element.589) | copy-start | bytes 3604
  24.0 356.9 %copy-start.144 = (f32[300]{0:T(512)}, f32[300]{0:T(512)S(1)}, u32[]{:S(2)}) copy-start(f32[300]{0:T(512)S(1)} %get-tuple-element.590) | copy-start | bytes 3604
  29.6 34.0 %copy-start.292 = (f32[4,100]{1,0:T(4,128)}, f32[4,100]{1,0:T(4,128)S(1)}, u32[]{:S(2)}) copy-start(f32[4,100]{1,0:T(4,128)S(1)} %get-tuple-element.433) | copy-start | bytes 4804
  29.6 34.7 %copy-start.291 = (f32[4,100]{1,0:T(4,128)}, f32[4,100]{1,0:T(4,128)S(1)}, u32[]{:S(2)}) copy-start(f32[4,100]{1,0:T(4,128)S(1)} %get-tuple-element.431) | copy-start | bytes 4804
  29.6 36.0 %copy-start.289 = (f32[4,100]{1,0:T(4,128)}, f32[4,100]{1,0:T(4,128)S(1)}, u32[]{:S(2)}) copy-start(f32[4,100]{1,0:T(4,128)S(1)} %get-tuple-element.427) | copy-start | bytes 4804
  29.6 36.6 %copy-start.242 = (f32[4,100]{1,0:T(4,128)}, f32[4,100]{1,0:T(4,128)S(1)}, u32[]{:S(2)}) copy-start(f32[4,100]{1,0:T(4,128)S(1)} %get-tuple-element.424) | copy-start | bytes 4804
  32.9 311.5 %copy-start.114 = (f32[12,25]{1,0:T(8,128)}, f32[12,25]{1,0:T(8,128)S(1)}, u32[]{:S(2)}) copy-start(f32[12,25]{1,0:T(8,128)S(1)} %add.1830) | copy-start | bytes 3604
  37.2 311.9 %copy-start.121 = (f32[1200]{0:T(1024)}, f32[1200]{0:T(1024)S(1)}, u32[]{:S(2)}) copy-start(f32[1200]{0:T(1024)S(1)} %convert_reduce_fusion.77) | copy-start | bytes 14404
  40.2 21.5 %copy-start.348 = (f32[4,100]{1,0:T(4,128)S(1)}, f32[4,100]{1,0:T(4,128)}, u32[]{:S(2)}) copy-start(f32[4,100]{1,0:T(4,128)} %get-tuple-element.432) | copy-start | bytes 4804
  40.2 29.2 %collective-permute-start = (bf16[4,300]{1,0:T(4,128)(2,1)}, bf16[4,300]{1,0:T(4,128)(2,1)}, u32[]{:S(2)}, u32[]{:S(2)}) collective-permute-start(bf16[4,300]{1,0:T(4,128)(2,1)} %get-tuple-element.423), channel_id=1, source_target_pairs={{0,16},{1,17},{2,18},{3,19},{4,20},{5,21},{6,22},{7,23},{8,24},{9,... | collective-permute-start | bytes 7208 | tf_op jit(solution)/shard_map/ppermute | solution.py:17
  70.0 40.0 %copy-start.178 = (bf16[4,300]{1,0:T(4,128)(2,1)}, bf16[4,300]{1,0:T(4,128)(2,1)S(1)}, u32[]{:S(2)}) copy-start(bf16[4,300]{1,0:T(4,128)(2,1)S(1)} %get-tuple-element.345) | copy-start | bytes 7204
  70.0 125.6 %copy-start.212 = (bf16[4,300]{1,0:T(4,128)(2,1)}, bf16[4,300]{1,0:T(4,128)(2,1)S(1)}, u32[]{:S(2)}) copy-start(bf16[4,300]{1,0:T(4,128)(2,1)S(1)} %get-tuple-element.344) | copy-start | bytes 7204
  81.6 12.5 %collective-permute-start.1 = (bf16[4,100,300]{2,1,0:T(8,128)(2,1)S(1)}, bf16[4,100,300]{2,1,0:T(8,128)(2,1)}, u32[]{:S(2)}, u32[]{:S(2)}) collective-permute-start(bf16[4,100,300]{2,1,0:T(8,128)(2,1)S(1)} %get-tuple-element.379), channel_id=1, source_target_pairs={{0,16},{1,17},{2,18},{3,19},{4,20},{5,21},{6,22},{7,23},{8,24},{9,... | collective-permute-start | bytes 720008 | tf_op jit(solution)/shard_map/ppermute | solution.py:17
  97.8 118.7 %copy-start.222 = (f32[4,100]{1,0:T(4,128)}, f32[4,100]{1,0:T(4,128)S(1)}, u32[]{:S(2)}) copy-start(f32[4,100]{1,0:T(4,128)S(1)} %broadcast_multiply_fusion.12) | copy-start | bytes 4804
  113.1 17.4 %collective-permute-start.3 = (bf16[4,300]{1,0:T(4,128)(2,1)}, bf16[4,300]{1,0:T(4,128)(2,1)}, u32[]{:S(2)}, u32[]{:S(2)}) collective-permute-start(bf16[4,300]{1,0:T(4,128)(2,1)} %get-tuple-element.422), channel_id=1, source_target_pairs={{0,16},{1,17},{2,18},{3,19},{4,20},{5,21},{6,22},{7,23},{8,24},{9,... | collective-permute-start | bytes 7208 | tf_op jit(solution)/shard_map/ppermute | solution.py:17
  124.5 14.3 %collective-permute-start.4 = (bf16[4,100,300]{2,1,0:T(8,128)(2,1)}, bf16[4,100,300]{2,1,0:T(8,128)(2,1)}, u32[]{:S(2)}, u32[]{:S(2)}) collective-permute-start(bf16[4,100,300]{2,1,0:T(8,128)(2,1)} %get-tuple-element.377), channel_id=1, source_target_pairs={{0,16},{1,17},{2,18},{3,19},{4,20},{5,21},{6,22},{7,23},{8,24},{9,... | collective-permute-start | bytes 720008 | tf_op jit(solution)/shard_map/ppermute | solution.py:17
  130.7 21.8 %copy-start.205 = (bf16[4,300]{1,0:T(4,128)(2,1)}, bf16[4,300]{1,0:T(4,128)(2,1)S(1)}, u32[]{:S(2)}) copy-start(bf16[4,300]{1,0:T(4,128)(2,1)S(1)} %get-tuple-element.319) | copy-start | bytes 7204
  155.5 18.6 %collective-permute-start.7 = (bf16[4,300]{1,0:T(4,128)(2,1)}, bf16[4,300]{1,0:T(4,128)(2,1)}, u32[]{:S(2)}, u32[]{:S(2)}) collective-permute-start(bf16[4,300]{1,0:T(4,128)(2,1)} %get-tuple-element.421), channel_id=1, source_target_pairs={{0,16},{1,17},{2,18},{3,19},{4,20},{5,21},{6,22},{7,23},{8,24},{9,... | collective-permute-start | bytes 7208 | tf_op jit(solution)/shard_map/ppermute | solution.py:17
  167.4 51.6 %collective-permute-start.8 = (bf16[4,100,300]{2,1,0:T(8,128)(2,1)}, bf16[4,100,300]{2,1,0:T(8,128)(2,1)}, u32[]{:S(2)}, u32[]{:S(2)}) collective-permute-start(bf16[4,100,300]{2,1,0:T(8,128)(2,1)} %get-tuple-element.375), channel_id=1, source_target_pairs={{0,16},{1,17},{2,18},{3,19},{4,20},{5,21},{6,22},{7,23},{8,24},{9,... | collective-permute-start | bytes 720008 | tf_op jit(solution)/shard_map/ppermute | solution.py:17
  174.2 56.4 %copy-start.210 = (bf16[4,300]{1,0:T(4,128)(2,1)}, bf16[4,300]{1,0:T(4,128)(2,1)S(1)}, u32[]{:S(2)}) copy-start(bf16[4,300]{1,0:T(4,128)(2,1)S(1)} %get-tuple-element.299) | copy-start | bytes 7204
  233.6 5.3 collective-permute-start.11
  240.3 108.7 %copy-start.180 = (bf16[4,300]{1,0:T(4,128)(2,1)}, bf16[4,300]{1,0:T(4,128)(2,1)S(1)}, u32[]{:S(2)}) copy-start(bf16[4,300]{1,0:T(4,128)(2,1)S(1)} %get-tuple-element.279) | copy-start | bytes 7204
  283.1 34.6 %collective-permute-start.12 = (bf16[4,100,300]{2,1,0:T(8,128)(2,1)}, bf16[4,100,300]{2,1,0:T(8,128)(2,1)}, u32[]{:S(2)}, u32[]{:S(2)}) collective-permute-start(bf16[4,100,300]{2,1,0:T(8,128)(2,1)} %get-tuple-element.373), channel_id=1, source_target_pairs={{0,16},{1,17},{2,18},{3,19},{4,20},{5,21},{6,22},{7,23},{8,24},{9,... | collective-permute-start | bytes 720008 | tf_op jit(solution)/shard_map/ppermute | solution.py:17
  346.2 20.9 %copy-start.19 = (bf16[4,100,300]{2,1,0:T(8,128)(2,1)S(1)}, bf16[4,100,300]{2,1,0:T(8,128)(2,1)}, u32[]{:S(2)}) copy-start(bf16[4,100,300]{2,1,0:T(8,128)(2,1)} %copy-done.17) | copy-start | bytes 720004
  352.2 28.7 %copy-start.249 = (bf16[4,300]{1,0:T(4,128)(2,1)}, bf16[4,300]{1,0:T(4,128)(2,1)S(1)}, u32[]{:S(2)}) copy-start(bf16[4,300]{1,0:T(4,128)(2,1)S(1)} %get-tuple-element.471) | copy-start | bytes 7204
  352.2 22.2 %copy-start.235 = (f32[4,300]{1,0:T(4,128)S(1)}, f32[4,300]{1,0:T(4,128)}, u32[]{:S(2)}) copy-start(f32[4,300]{1,0:T(4,128)} %get-tuple-element.339) | copy-start | bytes 14404
  352.2 24.3 %copy-start.266 = (bf16[4,300]{1,0:T(4,128)(2,1)S(1)}, bf16[4,300]{1,0:T(4,128)(2,1)}, u32[]{:S(2)}) copy-start(bf16[4,300]{1,0:T(4,128)(2,1)} %get-tuple-element.473) | copy-start | bytes 7204
  355.7 101.5 %collective-permute-start.16 = (bf16[4,100,300]{2,1,0:T(8,128)(2,1)}, bf16[4,100,300]{2,1,0:T(8,128)(2,1)}, u32[]{:S(2)}, u32[]{:S(2)}) collective-permute-start(bf16[4,100,300]{2,1,0:T(8,128)(2,1)} %get-tuple-element.371), channel_id=1, source_target_pairs={{0,16},{1,17},{2,18},{3,19},{4,20},{5,21},{6,22},{7,23},{8,24},{9,... | collective-permute-start | bytes 720008 | tf_op jit(solution)/shard_map/ppermute | solution.py:17
  362.5 11.9 %collective-permute-start.15 = (bf16[4,300]{1,0:T(4,128)(2,1)}, bf16[4,300]{1,0:T(4,128)(2,1)}, u32[]{:S(2)}, u32[]{:S(2)}) collective-permute-start(bf16[4,300]{1,0:T(4,128)(2,1)} %get-tuple-element.419), channel_id=1, source_target_pairs={{0,16},{1,17},{2,18},{3,19},{4,20},{5,21},{6,22},{7,23},{8,24},{9,... | collective-permute-start | bytes 7208 | tf_op jit(solution)/shard_map/ppermute | solution.py:17
  369.3 91.1 %collective-permute-start.5 = (bf16[4,100,300]{2,1,0:T(8,128)(2,1)}, bf16[4,100,300]{2,1,0:T(8,128)(2,1)}, u32[]{:S(2)}, u32[]{:S(2)}) collective-permute-start(bf16[4,100,300]{2,1,0:T(8,128)(2,1)} %fusion.368), channel_id=1, source_target_pairs={{16,0},{17,1},{18,2},{19,3},{20,4},{21,5},{22,6},{23,7},{24,8},{25... | collective-permute-start | bytes 720008 | tf_op jit(solution)/shard_map/ppermute | solution.py:17
  397.7 12.4 %collective-permute-start.2 = (bf16[4,300]{1,0:T(4,128)(2,1)}, bf16[4,300]{1,0:T(4,128)(2,1)S(1)}, u32[]{:S(2)}, u32[]{:S(2)}) collective-permute-start(bf16[4,300]{1,0:T(4,128)(2,1)} %get-tuple-element.411), channel_id=1, source_target_pairs={{16,0},{17,1},{18,2},{19,3},{20,4},{21,5},{22,6},{23,7},{24,8},{25... | collective-permute-start | bytes 7208 | tf_op jit(solution)/shard_map/ppermute | solution.py:17
  410.7 36.9 %copy-start.262 = (bf16[4,300]{1,0:T(4,128)(2,1)}, bf16[4,300]{1,0:T(4,128)(2,1)S(1)}, u32[]{:S(2)}) copy-start(bf16[4,300]{1,0:T(4,128)(2,1)S(1)} %get-tuple-element.167) | copy-start | bytes 7204
  488.2 114.6 %collective-permute-start.20 = (bf16[4,100,300]{2,1,0:T(8,128)(2,1)}, bf16[4,100,300]{2,1,0:T(8,128)(2,1)}, u32[]{:S(2)}, u32[]{:S(2)}) collective-permute-start(bf16[4,100,300]{2,1,0:T(8,128)(2,1)} %get-tuple-element.369), channel_id=1, source_target_pairs={{0,16},{1,17},{2,18},{3,19},{4,20},{5,21},{6,22},{7,23},{8,24},{9,... | collective-permute-start | bytes 720008 | tf_op jit(solution)/shard_map/ppermute | solution.py:17
  499.9 26.6 %copy-start.227 = (f32[4,100]{1,0:T(4,128)S(1)}, f32[4,100]{1,0:T(4,128)}, u32[]{:S(2)}) copy-start(f32[4,100]{1,0:T(4,128)} %copy-done.225) | copy-start | bytes 4804
  506.0 24.3 %copy-start.408 = (f32[300]{0:T(512)S(1)}, f32[300]{0:T(512)}, u32[]{:S(2)}) copy-start(f32[300]{0:T(512)} %get-tuple-element.543) | copy-start | bytes 3604
  506.0 24.3 %copy-start.407 = (f32[300]{0:T(512)S(1)}, f32[300]{0:T(512)}, u32[]{:S(2)}) copy-start(f32[300]{0:T(512)} %get-tuple-element.168) | copy-start | bytes 3604
  506.0 29.9 %copy-start.181 = (bf16[4,300]{1,0:T(4,128)(2,1)S(1)}, bf16[4,300]{1,0:T(4,128)(2,1)}, u32[]{:S(2)}) copy-start(bf16[4,300]{1,0:T(4,128)(2,1)} %copy-done.180) | copy-start | bytes 7204
  506.0 30.9 %copy-start.170 = (f32[300]{0:T(512)S(1)}, f32[300]{0:T(512)}, u32[]{:S(2)}) copy-start(f32[300]{0:T(512)} %copy-done.169) | copy-start | bytes 3604
  506.0 30.9 %copy-start.250 = (bf16[4,300]{1,0:T(4,128)(2,1)S(1)}, bf16[4,300]{1,0:T(4,128)(2,1)}, u32[]{:S(2)}) copy-start(bf16[4,300]{1,0:T(4,128)(2,1)} %copy-done.249) | copy-start | bytes 7204
  506.0 30.9 %copy-start.253 = (bf16[4,300]{1,0:T(4,128)(2,1)S(1)}, bf16[4,300]{1,0:T(4,128)(2,1)}, u32[]{:S(2)}) copy-start(bf16[4,300]{1,0:T(4,128)(2,1)} %get-tuple-element.467) | copy-start | bytes 7204
  506.0 28.7 %collective-permute-start.19 = (bf16[4,300]{1,0:T(4,128)(2,1)}, bf16[4,300]{1,0:T(4,128)(2,1)}, u32[]{:S(2)}, u32[]{:S(2)}) collective-permute-start(bf16[4,300]{1,0:T(4,128)(2,1)} %get-tuple-element.418), channel_id=1, source_target_pairs={{0,16},{1,17},{2,18},{3,19},{4,20},{5,21},{6,22},{7,23},{8,24},{9,... | collective-permute-start | bytes 7208 | tf_op jit(solution)/shard_map/ppermute | solution.py:17
  508.7 30.6 %copy-start.145 = (f32[300]{0:T(512)S(1)}, f32[300]{0:T(512)}, u32[]{:S(2)}) copy-start(f32[300]{0:T(512)} %copy-done.144) | copy-start | bytes 3604
  514.0 22.9 %copy-start.256 = (bf16[4,300]{1,0:T(4,128)(2,1)S(1)}, bf16[4,300]{1,0:T(4,128)(2,1)}, u32[]{:S(2)}) copy-start(bf16[4,300]{1,0:T(4,128)(2,1)} %get-tuple-element.469) | copy-start | bytes 7204
  514.0 20.7 %collective-permute-start.6 = (bf16[4,300]{1,0:T(4,128)(2,1)}, bf16[4,300]{1,0:T(4,128)(2,1)S(1)}, u32[]{:S(2)}, u32[]{:S(2)}) collective-permute-start(bf16[4,300]{1,0:T(4,128)(2,1)} %get-tuple-element.323), channel_id=1, source_target_pairs={{16,0},{17,1},{18,2},{19,3},{20,4},{21,5},{22,6},{23,7},{24,8},{25... | collective-permute-start | bytes 7208 | tf_op jit(solution)/shard_map/ppermute | solution.py:17
  528.9 167.2 %collective-permute-start.9 = (bf16[4,100,300]{2,1,0:T(8,128)(2,1)}, bf16[4,100,300]{2,1,0:T(8,128)(2,1)}, u32[]{:S(2)}, u32[]{:S(2)}) collective-permute-start(bf16[4,100,300]{2,1,0:T(8,128)(2,1)} %get-tuple-element.225), channel_id=1, source_target_pairs={{16,0},{17,1},{18,2},{19,3},{20,4},{21,5},{22,6},{23,7},{24,8},{25... | collective-permute-start | bytes 720008 | tf_op jit(solution)/shard_map/ppermute | solution.py:17
  552.1 24.2 %copy-start.45 = (bf16[4,1,12,25]{1,3,2,0:T(8,128)(2,1)}, bf16[4,1,12,25]{1,3,2,0:T(8,128)(2,1)S(1)}, u32[]{:S(2)}) copy-start(bf16[4,1,12,25]{1,3,2,0:T(8,128)(2,1)S(1)} %copy.713) | copy-start | bytes 7204
  639.9 31.3 %copy-start.228 = (f32[4,100]{1,0:T(4,128)}, f32[4,100]{1,0:T(4,128)S(1)}, u32[]{:S(2)}) copy-start(f32[4,100]{1,0:T(4,128)S(1)} %broadcast_multiply_fusion.8) | copy-start | bytes 4804
  691.7 46.8 %copy-start.403 = (f32[4]{0:T(128)}, f32[4]{0:T(128)S(1)}, u32[]{:S(2)}) copy-start(f32[4]{0:T(128)S(1)} %broadcast_multiply_fusion.26) | copy-start | bytes 52
  691.9 46.6 %copy-start.461 = (f32[4]{0:T(128)}, f32[4]{0:T(128)S(1)}, u32[]{:S(2)}) copy-start(f32[4]{0:T(128)S(1)} %fusion.1375) | copy-start | bytes 52
  696.1 39.6 %copy-start.201 = (f32[4,1200]{1,0:T(4,128)}, f32[4,1200]{1,0:T(4,128)S(1)}, u32[]{:S(2)}) copy-start(f32[4,1200]{1,0:T(4,128)S(1)} %convolution_add_fusion.6) | copy-start | bytes 57604
  718.5 16.5 %collective-permute-start.10 = (bf16[4,300]{1,0:T(4,128)(2,1)S(1)}, bf16[4,300]{1,0:T(4,128)(2,1)S(1)}, u32[]{:S(2)}, u32[]{:S(2)}) collective-permute-start(bf16[4,300]{1,0:T(4,128)(2,1)S(1)} %get-tuple-element.303), channel_id=1, source_target_pairs={{16,0},{17,1},{18,2},{19,3},{20,4},{21,5},{22,6},{23,7},{24,8},{25... | collective-permute-start | bytes 7208 | tf_op jit(solution)/shard_map/ppermute | solution.py:17
  722.4 46.8 %collective-permute-start.13 = (bf16[4,100,300]{2,1,0:T(8,128)(2,1)}, bf16[4,100,300]{2,1,0:T(8,128)(2,1)}, u32[]{:S(2)}, u32[]{:S(2)}) collective-permute-start(bf16[4,100,300]{2,1,0:T(8,128)(2,1)} %get-tuple-element.223), channel_id=1, source_target_pairs={{16,0},{17,1},{18,2},{19,3},{20,4},{21,5},{22,6},{23,7},{24,8},{25... | collective-permute-start | bytes 720008 | tf_op jit(solution)/shard_map/ppermute | solution.py:17
  786.7 8.2 collective-permute-start.14
  791.6 36.8 %collective-permute-start.17 = (bf16[4,100,300]{2,1,0:T(8,128)(2,1)}, bf16[4,100,300]{2,1,0:T(8,128)(2,1)}, u32[]{:S(2)}, u32[]{:S(2)}) collective-permute-start(bf16[4,100,300]{2,1,0:T(8,128)(2,1)} %get-tuple-element.221), channel_id=1, source_target_pairs={{16,0},{17,1},{18,2},{19,3},{20,4},{21,5},{22,6},{23,7},{24,8},{25... | collective-permute-start | bytes 720008 | tf_op jit(solution)/shard_map/ppermute | solution.py:17
  845.8 8.4 collective-permute-start.18
  850.8 35.3 %collective-permute-start.21 = (bf16[4,100,300]{2,1,0:T(8,128)(2,1)}, bf16[4,100,300]{2,1,0:T(8,128)(2,1)}, u32[]{:S(2)}, u32[]{:S(2)}) collective-permute-start(bf16[4,100,300]{2,1,0:T(8,128)(2,1)} %get-tuple-element.219), channel_id=1, source_target_pairs={{16,0},{17,1},{18,2},{19,3},{20,4},{21,5},{22,6},{23,7},{24,8},{25... | collective-permute-start | bytes 720008 | tf_op jit(solution)/shard_map/ppermute | solution.py:17
  903.5 8.2 collective-permute-start.22
  908.5 42.0 %collective-permute-start.23 = (bf16[4,100,300]{2,1,0:T(8,128)(2,1)}, bf16[4,100,300]{2,1,0:T(8,128)(2,1)}, u32[]{:S(2)}, u32[]{:S(2)}) collective-permute-start(bf16[4,100,300]{2,1,0:T(8,128)(2,1)} %get-tuple-element.217), channel_id=1, source_target_pairs={{16,0},{17,1},{18,2},{19,3},{20,4},{21,5},{22,6},{23,7},{24,8},{25... | collective-permute-start | bytes 720008 | tf_op jit(solution)/shard_map/ppermute | solution.py:17
  (514 other events, 2885.1 us)
Sparse Core Ops, SparseCore 0:
  967.5 131.8 all-reduce.17
where the time goes:
time: 1140 us; the launch traced here: 1120 us
  matrix products  354 us (31%)
  local copies, waits for them, and re-layouts  344 us (30%)
  other arithmetic  226 us (20%)
  blocking collectives  62.6 us (5%)
  waiting for transfers between devices  60 us (5%)
  starting transfers between devices  49 us (4%)
  between operations  21 us (2%)
    dot_general x105, matrix products, product(): return jnp.dot(operand, factor, preferred_element_type=jnp.float32)  122 us
    dot_general x63, matrix products, outer_sum(): jnp.einsum('na,nb->ab', operand, factor, preferred_element_type=jnp.float32)  110 us
    dot_general x63, matrix products, against(): jnp.einsum('na,ba->nb', operand, factor, preferred_element_type=jnp.float32)  73.5 us
    psum x1, blocking collectives, on_device(): lax.psum((partial_value[0], partial_value[1], partial_value[2], partial_v...  62.6 us
    psum x1, waiting for transfers between devices, on_device(): lax.psum((partial_value[0], partial_value[1], partial_value[2], partial_v...  59.9 us
    ppermute x24, starting transfers between devices, passed_along(): return lax.ppermute(block, axis, route)  49 us
    dot_general x30, local copies, waits for them, and re-layouts, product(): return jnp.dot(operand, factor, preferred_element_type=jnp.float32)  48.9 us
    unnamed x1112, local copies, waits for them, and re-layouts  33.5 us
  transfers between devices with their start and end apart: 25, of which 1 were waited for; matrix products, arithmetic and copies ran while one was open for 54% of the time, Pallas kernels for 0%

commit v1 on v0

v1 whole, which is shorter than its diff:
```python
import functools
import math

import jax
import jax.numpy as jnp
from jax import lax
from jax.experimental import pallas as pl
from jax.experimental.pallas import tpu as pltpu
from jax.sharding import PartitionSpec as P

HEADS = 12
HEAD_ROWS = 16
TILE = 8
PAIR = 16
PIECES = 5
LOADS = 4
FIRST_PIECES = 2
MOST_GATHERED = 16
EPSILON = 1e-05
MASKED_SCORE = -1e30
F32 = jnp.float32
BF16 = jnp.bfloat16
MESH_ID = pl.DeviceIdType.MESH


def padded(size):
    return -(-size // 128) * 128


def split_devices(count):
    radices = []
    for _ in range(2):
        if count % 2 == 0 and count > 1:
            radices.append(2)
            count //= 2
    return radices + [count] if count > 1 else radices


def aligned(start):
    return start if isinstance(start, int) else pl.multiple_of(start, PAIR)


def product(operand, factor):
    return lax.dot_general(
        operand, factor, (((1,), (0,)), ((), ())), preferred_element_type=F32
    )


def against(operand, factor):
    return lax.dot_general(
        operand, factor, (((1,), (1,)), ((), ())), preferred_element_type=F32
    )


def outer_sum(operand, factor):
    return lax.dot_general(
        operand, factor, (((0,), (0,)), ((), ())), preferred_element_type=F32
    )


def low(values):
    return values.astype(BF16)


def wide(values):
    return values.astype(F32)


def gelu_parts(values):
    phi = 0.5 * (1.0 + lax.erf(values * (0.5**0.5)))
    density = jnp.exp(-0.5 * values * values) * 0.3989422804014327
    return values * phi, phi + values * density


def sum_pairs(values):
    return values[:TILE] + values[TILE:]


def pad_rows(values):
    return jnp.concatenate([values, jnp.zeros_like(values)], 0)


def flat(values):
    return values.reshape(values.shape[0] * values.shape[1], values.shape[2])


class Sizes:
    def __init__(self, star_count, slot_count, model_width, hidden_width, devices):
        self.stars = star_count
        self.slots = slot_count
        self.width = model_width
        self.hidden = hidden_width
        self.devices = devices
        self.lanes = padded(model_width)
        self.hidden_lanes = padded(hidden_width)
        self.main = self.lanes - 128
        self.groups = star_count // TILE
        self.rows = slot_count * TILE
        self.piece = self.rows // PIECES
        tall = -(-self.piece // 3 // PAIR) * PAIR
        self.short = (self.piece - tall) // 2
        self.tall = tall
        self.over = model_width - self.main
        self.fits = 128 - 2 * self.over
        self.spill = self.over - self.fits
        assert self.short % PAIR == 0 and tall - self.short == PAIR and self.spill > 0
        assert self.short // PAIR * self.spill <= self.fits
        self.within = devices <= MOST_GATHERED
        self.radices = split_devices(devices) if self.within else []
        self.gathers = devices if self.within else 1
        self.factor_lanes = 3 * self.lanes + self.hidden_lanes
        self.blocks = self.groups * self.gathers
        self.side_rows = -(-self.blocks // 2) * PAIR
        self.block = -(-(model_width + 1) // TILE) * TILE
        self.sum_rows = 256
        self.spare = self.lanes - model_width
        self.sum_parts = -(-model_width // self.spare)
        self.sum_part = self.sum_rows // self.sum_parts
        self.extra_at = self.block - self.sum_rows
        assert self.extra_at % TILE == 0 and self.extra_at + 6 <= self.sum_part
        assert self.sum_rows % (PAIR * self.gathers) == 0
        assert 3 * self.lanes <= self.hidden_lanes

    def shift(self, part):
        return (self.width - part * self.spare) % self.lanes


def scattered(total, radices):
    return [total // math.prod(radices[:k]) for k in range(len(radices))]


def flattened(radices):
    return radices[:1] + ([math.prod(radices[1:])] if len(radices) > 1 else [])


class Peers:
    def __init__(self, radices):
        self.radices = radices
        self.last = len(radices) - 1
        self.strides = [math.prod(radices[:k]) for k in range(len(radices))]
        self.at = lax.axis_index("dp")
        self.digits = [
            (self.at // stride) % radix for stride, radix in zip(self.strides, radices)
        ]

    def other(self, stage, distance):
        digit = (self.digits[stage] + distance) % self.radices[stage]
        return digit, {"dp": self.at + (digit - self.digits[stage]) * self.strides[stage]}

    def everyone(self):
        return [
            self.other(stage, distance)[1]
            for stage in range(len(self.radices))
            for distance in range(1, self.radices[stage])
        ]

    def copies(self, stage, source, target, sends, receives):
        found = []
        for distance in range(1, self.radices[stage]):
            digit, device = self.other(stage, distance)
            found.append(
                pltpu.make_async_remote_copy(
                    src_ref=source(digit),
                    dst_ref=target(distance),
                    send_sem=sends.at[stage, distance - 1],
                    recv_sem=receives.at[stage, distance - 1],
                    device_id=device,
                    device_id_type=MESH_ID,
                )
            )
        return found

    def first(self, stage):
        return sum(
            self.digits[k] * math.prod(self.radices[k + 1 :]) for k in range(stage + 1)
        )


class Gather:
    def __init__(self, peers, blocks, group, sems):
        self.peers, self.blocks, self.group = peers, blocks, group
        self.sends, self.receives = sems.at[0, group], sems.at[1, group]
        self.count = math.prod(peers.radices)

    def copies(self, stage):
        size = math.prod(self.peers.radices[stage + 1 :])
        place = self.blocks.at[pl.ds(self.group * self.count + self.peers.first(stage), size)]
        return self.peers.copies(
            stage, lambda digit: place, lambda distance: place, self.sends, self.receives
        )

    def push(self, stage):
        if stage < self.peers.last:
            self.finish(stage + 1)
        for copy in self.copies(stage):
            copy.start()

    def finish(self, stage):
        for copy in self.copies(stage):
            copy.wait_recv()

    def drain(self):
        for stage in range(self.peers.last + 1):
            for copy in self.copies(stage):
                copy.wait_send()


class Reduction:
    def __init__(self, peers, total, total_low, outgoing, incoming, sems):
        self.peers, self.total, self.total_low = peers, total, total_low
        self.outgoing, self.incoming = outgoing, incoming
        self.scatter_sems, self.share_sems = sems[:2], sems[2:]
        self.stages = peers.last + 1
        self.steps = 2 * self.stages + 1

    def region(self, stage):
        start, length = 0, self.total.shape[0]
        for k in range(stage):
            length //= self.peers.radices[k]
            start = start + self.peers.digits[k] * length
        return start, length

    def scatter_copies(self, stage):
        part = self.region(stage)[1] // self.peers.radices[stage]
        return self.peers.copies(
            stage,
            lambda digit: self.outgoing[stage].at[pl.ds(aligned(digit * part), part)],
            lambda distance: self.incoming[stage].at[distance - 1],
            *self.scatter_sems,
        )

    def share_copies(self, stage):
        start, length = self.region(stage + 1)
        place = self.total_low.at[pl.ds(aligned(start), length)]
        return self.peers.copies(
            stage, lambda digit: place, lambda distance: place, *self.share_sems
        )

    def step(self, at):
        if 1 <= at <= self.stages:
            start, length = self.region(at)
            place = pl.ds(aligned(start), length)
            for index, copy in enumerate(self.scatter_copies(at - 1)):
                copy.wait_recv()
                self.total[place, :] += wide(self.incoming[at - 1][index])
        if at < self.stages:
            start, length = self.region(at)
            self.outgoing[at][...] = low(self.total[pl.ds(aligned(start), length), :])
            for copy in self.scatter_copies(at):
                copy.start()
            return
        if at == self.stages:
            start, length = self.region(at)
            place = pl.ds(aligned(start), length)
            self.total_low[place, :] = low(self.total[place, :])
        else:
            for copy in self.share_copies(2 * self.stages - at):
                copy.wait_recv()
        stage = 2 * self.stages - 1 - at
        if stage >= 0:
            for copy in self.share_copies(stage):
                copy.start()

    def drain(self):
        for stage in range(self.stages):
            for copy in self.scatter_copies(stage) + self.share_copies(stage):
                copy.wait_send()


class LateReduction:
    def __init__(self, near, total, total_low, handed, got, outgoing, incoming, sems):
        self.near, self.total, self.total_low = near, total, total_low
        self.handed, self.got, self.outgoing, self.incoming = handed, got, outgoing, incoming
        self.hand_sems, self.back_sems, self.scatter_sems, self.share_sems = (
            sems[:2], sems[2:4], sems[4:6], sems[6:]
        )
        self.odd = near.digits[0] == 1
        self.chips = near.radices[1] if near.last > 0 else 1
        self.part = total.shape[0] // self.chips

    def hand(self):
        return self.near.copies(
            0, lambda digit: self.handed, lambda distance: self.got, *self.hand_sems
        )[0]

    def back(self):
        return self.near.copies(
            0, lambda digit: self.total_low, lambda distance: self.total_low, *self.back_sems
        )[0]

    def place(self, digit):
        return pl.ds(aligned(digit * self.part), self.part)

    def scatter(self):
        if self.chips == 1:
            return []
        return self.near.copies(
            1,
            lambda digit: self.outgoing.at[self.place(digit)],
            lambda distance: self.incoming.at[distance - 1],
            *self.scatter_sems,
        )

    def share(self):
        if self.chips == 1:
            return []
        own = self.total_low.at[self.place(self.near.digits[1])]
        return self.near.copies(
            1, lambda digit: own, lambda distance: own, *self.share_sems
        )

    def step(self, at):
        if at == 0:

            @pl.when(jnp.logical_not(self.odd))
            def _():
                self.handed[...] = low(self.total[...])
                self.hand().start()

            @pl.when(self.odd)
            def _():
                self.hand().wait_recv()
                self.total[...] += wide(self.got[...])
                self.outgoing[...] = low(self.total[...])
                for copy in self.scatter():
                    copy.start()

        elif at == 1:

            @pl.when(self.odd)
            def _():
                own = self.place(self.near.digits[1] if self.chips > 1 else 0)
                chunk = self.total[own, :]
                for index, copy in enumerate(self.scatter()):
                    copy.wait_recv()
                    chunk = chunk + wide(self.incoming[index])
                self.total_low[own, :] = low(chunk)
                for copy in self.share():
                    copy.start()

        elif at == 2:

            @pl.when(self.odd)
            def _():
                for copy in self.share():
                    copy.wait_recv()
                self.back().start()

        elif at == 3:
            pl.when(jnp.logical_not(self.odd))(lambda: self.back().wait_recv())

    steps = 4

    def drain(self):
        @pl.when(jnp.logical_not(self.odd))
        def _():
            self.hand().wait_send()

        @pl.when(self.odd)
        def _():
            self.back().wait_send()
            for copy in self.scatter() + self.share():
                copy.wait_send()


def layer_kernel(
    z,
    center_ref,
    edge_far,
    counts_ref,
    mask_ref,
    square_far,
    out_far,
    up_far,
    down_far,
    gain_ref,
    bias_ref,
    hidden_ref,
    center_result,
    final_result,
    left_side,
    right_side,
    key_low,
    value_low,
    edge_low,
    norm_result,
    final,
    left_keep,
    right_keep,
    layer_in,
    cotangent,
    got_main,
    got_tail,
    sent_main,
    sent_tail,
    got_center,
    sent_center,
    layer_center,
    normed,
    gated,
    live_grad,
    gate_grad,
    mean_keep,
    scale_keep,
    live_rows,
    live_lanes,
    allowed,
    prob_keep,
    prob_low,
    wide_a,
    wide_b,
    wide_c,
    staging,
    square_rows,
    score_low,
    w_query,
    w_key,
    w_value,
    w_edge,
    w_out,
    w_up,
    w_down,
    rows_keep,
    query_keep,
    key_keep,
    context_keep,
    value_keep,
    score_keep,
    center_low,
    center_wide,
    center_scale,
    hidden_low,
    hidden_wide,
    middle_keep,
    feed_keep,
    row_sums,
    edge_weight_sum,
    left_blocks,
    right_blocks,
    key_sum,
    value_sum,
    edge_sum,
    key_pass,
    value_pass,
    edge_pass,
    send_sem,
    recv_sem,
    center_sem,
    left_sems,
    right_sems,
    key_sems,
    value_sems,
    edge_sems,
    side_sem,
    final_sem,
    turn_sem,
    edge_ref,
    square_ref,
    out_ref,
    up_ref,
    down_ref,
    load_sem,
):
    lanes, width, groups, rows, piece = z.lanes, z.width, z.groups, z.rows, z.piece
    head_size = width // HEADS
    scaling = head_size**-0.5
    inverse = 1.0 / width
    me = lax.axis_index("section")
    partner = {"section": 1 - me}
    peers = Peers(z.radices)
    near = Peers(flattened(z.radices))
    last = peers.last
    turns = z.within and z.radices[:1] == [2] and groups == 3
    core = peers.digits[0] if turns else 0

    share = z.slots // LOADS
    edge_loads = [
        pltpu.make_async_copy(
            edge_far.at[pl.ds(k * share, share)],
            edge_ref.at[pl.ds(k * share, share)],
            load_sem.at[k],
        )
        for k in range(LOADS)
    ]
    weight_loads = [
        pltpu.make_async_copy(source, target, load_sem.at[LOADS + k])
        for k, (source, target) in enumerate(
            (
                (square_far, square_ref),
                (out_far, out_ref),
                (up_far, up_ref),
                (down_far, down_ref),
            )
        )
    ]
    for load in edge_loads + weight_loads:
        load.start()

    barrier = pltpu.get_barrier_semaphore()
    neighbours = [partner] + near.everyone()
    for neighbour in neighbours:
        pl.semaphore_signal(barrier, inc=1, device_id=neighbour, device_id_type=MESH_ID)

    lane = lax.broadcasted_iota(jnp.int32, (1, lanes), 1)
    inside = (lane < width).astype(F32)
    one_lane = (lane == width).astype(F32)
    head_row = lax.broadcasted_iota(jnp.int32, (HEAD_ROWS, lanes), 0)
    head_lane = lax.broadcasted_iota(jnp.int32, (HEAD_ROWS, lanes), 1)
    head_mask = (
        (head_lane >= head_row * head_size)
        & (head_lane < head_row * head_size + head_size)
        & (head_row < HEADS)
    ).astype(F32)
    star_lane = lax.broadcasted_iota(jnp.int32, (TILE, 128), 1)
    star_row = lax.broadcasted_iota(jnp.int32, (TILE, 128), 0)
    own_star = (
        (star_lane >= star_row * HEAD_ROWS) & (star_lane < star_row * HEAD_ROWS + HEAD_ROWS)
    ).astype(F32)
    tail_lane = lax.broadcasted_iota(jnp.int32, (1, 128), 1)

    full = width // PAIR * PAIR

    def prepare(target, first, rest, bias_row):
        count = target.shape[1]
        target[:full, count - 128 :] = jnp.zeros((full, 128), BF16)
        target[:full, : first.shape[1]] = first
        staging[:PAIR, :count] = jnp.zeros((PAIR, count), F32)
        staging[: width - full, : rest.shape[1]] = wide(rest)
        if bias_row is not None:
            staging[width - full : width - full + 1, : bias_row.shape[1]] = wide(bias_row)
        target[full : full + PAIR, :] = low(staging[:PAIR, :count])
        target[full + PAIR :, :] = jnp.zeros((lanes - full - PAIR, count), BF16)

    def prepare_square(target, index, bias_row):
        def strided(start, count):
            return jnp.concatenate(
                [part[pl.ds(start, count, stride=4), :] for part in square_rows], 1
            )[:, :width]

        first = low(strided(index, full))
        rest = strided(index + 4 * full, width - full)
        prepare(target, first, rest, bias_row)

    def take_apart():
        def one(at, carry):
            place = pl.ds(pl.multiple_of(at * TILE, TILE), TILE)
            both = jnp.concatenate([wide(square_ref[2 * at]), wide(square_ref[2 * at + 1])], 0)
            for index, part in enumerate(square_rows):
                piece_lanes = both[:, index * 128 : (index + 1) * 128]
                part[place, : piece_lanes.shape[1]] = piece_lanes
            return carry

        lax.fori_loop(0, width // 2, one, 0, unroll=10)

    def prepare_first():
        weight_loads[0].wait()
        take_apart()
        prepare_square(w_edge, 3, bias_ref[6:7, :])

    def prepare_rest():
        prepare_square(w_query, 0, bias_ref[3:4, :])
        prepare_square(w_key, 1, None)
        prepare_square(w_value, 2, bias_ref[4:5, :])
        for load in weight_loads[1:]:
            load.wait()
        prepare(w_out, out_ref[:full, :], out_ref[full:, :], bias_ref[5:6, :])
        prepare(w_up, up_ref[:full, :], up_ref[full:, :], hidden_ref[...])
        prepare(w_down, down_ref[:full, :], down_ref[full:, :], None)

    rows_keep[...] = jnp.zeros((TILE, lanes), F32)
    rows_keep[0:3, :width] = wide(gain_ref[...])
    rows_keep[3:6, :width] = wide(bias_ref[0:3, :])
    rows_keep[6:7, :width] = wide(bias_ref[7:8, :])
    gain_center = rows_keep[0:1, :]
    gain_edge = rows_keep[1:2, :]
    gain_feed = rows_keep[2:3, :]
    bias_center = rows_keep[3:4, :] + one_lane
    bias_edge = rows_keep[4:5, :] + one_lane
    bias_feed = rows_keep[5:6, :] + one_lane
    bias_down = rows_keep[6:7, :]
    row_sums[...] = jnp.zeros((6, TILE, lanes), F32)
    edge_weight_sum[...] = jnp.zeros((lanes, lanes), F32)

    def unpack_own(target):
        def one(at, carry):
            first = wide(edge_ref[2 * at])
            second = wide(edge_ref[2 * at + 1])
            place = pl.ds(pl.multiple_of(at * PAIR, PAIR), PAIR)
            for group in range(groups):
                part = slice(group * TILE, (group + 1) * TILE)
                target[group, place, :width] = low(
                    jnp.concatenate([first[part], second[part]], 0)
                )
            return carry

        for group in range(groups):
            target[group, :, z.main :] = jnp.zeros((rows, 128), BF16)
        for load in edge_loads:
            load.wait()
        lax.fori_loop(0, z.slots // 2, one, 0, unroll=5)

    def unpack_center(target):
        staging[: z.stars, :lanes] = jnp.zeros((z.stars, lanes), F32)
        staging[: z.stars, :width] = wide(center_ref[...])
        for group in range(groups):
            target[group] = low(pad_rows(staging[group * TILE : (group + 1) * TILE, :lanes]))

    def find_live():
        counts = jnp.zeros((z.stars, z.slots), jnp.int32)
        star_at = lax.broadcasted_iota(jnp.int32, (z.stars, z.slots), 0)
        slot_at = lax.broadcasted_iota(jnp.int32, (z.stars, z.slots), 1)
        for star in range(z.stars):
            counts = jnp.where(star_at == star, counts_ref[star], counts)
        live = ((slot_at < counts) & (mask_ref[...] > 0)).astype(F32)
        spread = low(pad_rows(own_star))
        slots = z.slots // PIECES
        for group in range(groups):
            part = low(pad_rows(live[group * TILE : (group + 1) * TILE]))
            turned = outer_sum(part, spread)
            for at in range(PIECES):
                live_lanes[group, at, :slots, :] = turned[at * slots : (at + 1) * slots]
            allowed[group, rows : rows + TILE, :] = own_star
            allowed[group, rows + TILE :, :] = jnp.zeros((TILE, 128), F32)

    blocks = [(0, z.tall), (z.tall, z.short), (z.tall + z.short, z.short)]

    def spans(at):
        return [pl.ds(pl.multiple_of(at * piece + start, PAIR), count) for start, count in blocks]

    def tail_span(at):
        return pl.ds(pl.multiple_of(at * z.tall, PAIR), z.tall)

    def cut_blocks(values):
        return [values[start : start + count] for start, count in blocks]

    def whole_span(at):
        return pl.ds(pl.multiple_of(at * piece, PAIR), piece)

    def three(column):
        return jnp.concatenate([column] * (lanes // 128), axis=1)

    def open_piece(group, at):
        count = piece // TILE
        slots = live_lanes[group, at][:count]
        here = (jnp.broadcast_to(slots[:, None, :], (count, TILE, 128)) * own_star[None]).reshape(
            piece, 128
        )
        allowed[group, whole_span(at), :] = here
        live_rows[group, whole_span(at), :] = jnp.broadcast_to(
            jnp.max(here, axis=1, keepdims=True), (piece, 128)
        )

    def normalise(values):
        mean = jnp.sum(values, axis=1, keepdims=True) * inverse
        centred = values - mean * inside
        spread = jnp.sum(centred * centred, axis=1, keepdims=True) * inverse
        scale = lax.rsqrt(spread + EPSILON)
        return centred * scale, mean, scale

    def norm_back(unit, scale, grad_unit):
        first = jnp.sum(grad_unit, axis=1, keepdims=True) * inverse
        second = jnp.sum(grad_unit * unit, axis=1, keepdims=True) * inverse
        return scale * (grad_unit - first - unit * second)

    def over_heads(values):
        return jnp.sum(values.reshape(TILE, HEAD_ROWS, lanes) * head_mask[None], axis=1)

    def by_head(values):
        return (values[:, None, :] * head_mask[None]).reshape(TILE * HEAD_ROWS, lanes)

    def piece_copies(group, at):
        main = whole_span(at)
        tail = tail_span(at)
        return [
            pltpu.make_async_remote_copy(
                src_ref=source.at[group, place],
                dst_ref=target.at[group, place],
                send_sem=send_sem.at[group, at, index],
                recv_sem=recv_sem.at[group, at, index],
                device_id=partner,
                device_id_type=MESH_ID,
            )
            for index, (source, target, place) in enumerate(
                ((sent_main, got_main, main), (sent_tail, got_tail, tail))
            )
        ]

    def center_copy(group):
        return pltpu.make_async_remote_copy(
            src_ref=sent_center.at[group],
            dst_ref=got_center.at[group],
            send_sem=center_sem.at[0, group],
            recv_sem=center_sem.at[1, group],
            device_id=partner,
            device_id_type=MESH_ID,
        )

    def only(values, first, count):
        return jnp.where((tail_lane >= first) & (tail_lane < first + count), values, 0.0)

    def put_blocks(group, at, values):
        for place, value in zip(spans(at), values):
            sent_main[group, place, :] = low(value[:, : z.main])
        first, second, third = [only(value[:, z.main :], 0, z.over) for value in values]
        start = 2 * z.over
        below = 0.0
        for k in range(z.short // PAIR):
            shift = start + k * z.spill
            part = pltpu.roll(third[k * PAIR : (k + 1) * PAIR], shift - z.fits, 1)
            below = below + only(part, shift, z.spill)
        beside = pltpu.roll(second, z.over, 1) + only(pltpu.roll(third, start, 1), start, z.fits)
        sent_tail[group, tail_span(at), :] = low(first + jnp.concatenate([beside, below], 0))

    def get_blocks(group, at):
        tail = wide(got_tail[group, tail_span(at), :])
        upper, lower = tail[: z.short], tail[z.short :]
        start = 2 * z.over
        spilt = jnp.concatenate(
            [
                only(pltpu.roll(lower, 128 - start - k * z.spill + z.fits, 1), z.fits, z.spill)
                for k in range(z.short // PAIR)
            ],
            0,
        )
        tails = [
            only(tail, 0, z.over),
            only(pltpu.roll(upper, 128 - z.over, 1), 0, z.over),
            only(pltpu.roll(upper, 128 - start, 1), 0, z.fits) + spilt,
        ]
        return [
            jnp.concatenate([wide(got_main[group, place, :]), part], 1)
            for place, part in zip(spans(at), tails)
        ]

    zero_tile = jnp.zeros((TILE, lanes), F32)

    def fold(values):
        return jnp.sum(values.reshape(values.shape[0] // TILE, TILE, lanes), axis=0)

    def repeated(values):
        return jnp.broadcast_to(
            values[:TILE][None], (z.tall // TILE, TILE, lanes)
        ).reshape(z.tall, lanes)

    def norm_center(group):
        center = wide(layer_center[group])
        unit, _, scale = normalise(center)
        center_norm = low(unit * gain_center + bias_center)
        center_low[0, group] = center_norm
        center_wide[0, group] = unit
        center_scale[0, group] = jnp.broadcast_to(scale, (PAIR, 128))
        normed[group, rows:, :] = low(pad_rows(wide(center_norm)[:TILE]))
        return center_norm

    def ask_center(group):
        query = low(product(center_low[0, group], w_query[...]))
        query_heads = low(by_head(wide(query)[:TILE]))
        query_keep[group] = query_heads
        key_keep[group] = low(against(query_heads, w_key[...]) * scaling)

    def norm_span(group, place, values):
        unit, mean, scale = normalise(values)
        mean_keep[group, place, :] = jnp.broadcast_to(mean, (values.shape[0], 128))
        scale_keep[group, place, :] = jnp.broadcast_to(scale, (values.shape[0], 128))
        edge_norm = low(unit * gain_edge + bias_edge)
        normed[group, place, :] = edge_norm
        return wide(edge_norm)

    def update_span(group, place, changed, values, sums):
        out_sum, update_sum = sums
        update = changed * three(live_rows[group, place, :])
        result = values + update
        return result, (out_sum + fold(result * result), update_sum + fold(update * update))

    def forward_center(group):
        scores = against(normed[group], key_keep[group])
        yield
        open_slots = allowed[group] > 0
        top = jnp.max(jnp.where(open_slots, scores, MASKED_SCORE), axis=0, keepdims=True)
        raised = jnp.where(open_slots, jnp.exp(scores - top), 0.0)
        probs = raised * (1.0 / jnp.sum(raised, axis=0, keepdims=True))
        prob_keep[group] = probs
        probs_low = low(probs)
        prob_low[group] = probs_low
        yield
        context = low(outer_sum(probs_low, normed[group]))
        yield
        context_keep[group] = context
        attended = low(pad_rows(over_heads(product(context, w_value[...]))) + one_lane)
        center_low[1, group] = attended
        yield
        branch_attn = product(attended, w_out[...])
        middle = wide(layer_center[group]) + branch_attn
        yield
        unit, _, scale = normalise(middle)
        center_wide[1, group] = unit
        center_scale[1, group] = jnp.broadcast_to(scale, (PAIR, 128))
        feed_norm = low(unit * gain_feed + bias_feed)
        center_low[2, group] = feed_norm
        hidden = product(feed_norm, w_up[...])
        hidden_wide[group] = hidden
        yield
        feed_keep[group] = middle

    def feed_center(group, target):
        middle = feed_keep[group]
        active = low(gelu_parts(hidden_wide[group])[0])
        hidden_low[0, group] = active
        branch_feed = against(active, w_down[...]) + bias_down
        yield
        center_out = middle + branch_feed
        target[group] = low(pad_rows(center_out[:TILE]))
        branch_attn = middle - wide(layer_center[group])
        for index, measure in ((0, center_out), (2, branch_attn), (4, branch_feed)):
            put_norm(group, index, (measure * measure)[:TILE], width)

    def put_norm(group, index, squares, count):
        measure = jnp.sqrt(jnp.sum(squares, axis=1, keepdims=True) * (1.0 / count))
        norm_result[group] = jnp.where(star_lane == index, measure, norm_result[group])

    def put_edge_norms(group, sums):
        out_sum, update_sum = sums
        put_norm(group, 1, out_sum, width * z.slots)
        put_norm(group, 3, update_sum, width * z.slots)

    def backward_center(group, grad_low):
        grad_center = wide(grad_low)
        center_low[3, group] = grad_low
        grad_active = product(grad_low, w_down[...])
        grad_hidden = low(gelu_parts(hidden_wide[group])[1] * grad_active)
        hidden_low[1, group] = grad_hidden
        yield
        grad_norm = against(grad_hidden, w_up[...])
        unit = center_wide[1, group]
        row_sums[2] += sum_pairs(grad_norm * unit)
        row_sums[5] += sum_pairs(grad_norm)
        grad_middle = grad_center + norm_back(
            unit, center_scale[1, group][:, :1], grad_norm * gain_feed
        )
        middle_keep[group] = grad_middle
        yield
        grad_attn = low(grad_middle)
        center_low[4, group] = grad_attn
        grad_attended = wide(low(against(grad_attn, w_out[...])))
        value_heads = low(by_head(grad_attended[:TILE]))
        value_keep[group] = value_heads
        yield
        value_map = low(against(value_heads, w_value[...]))
        yield
        probs = prob_keep[group]
        weighted = probs * against(normed[group], value_map)
        grad_scores = low(weighted - probs * jnp.sum(weighted, axis=0, keepdims=True))
        wide_b[...] = product(
            jnp.concatenate([prob_low[group], grad_scores], 1),
            jnp.concatenate([value_map, key_keep[group]], 0),
        )
        score_low[...] = grad_scores

    def score_center(group):
        score_sum = low(outer_sum(score_low[...], normed[group]))
        score_keep[group] = score_sum
        yield
        grad_query = low(pad_rows(over_heads(product(score_sum, w_key[...]))) * scaling)
        center_low[5, group] = grad_query
        yield

    def finish_center(group, center_sum, target):
        yield
        grad_norm = (
            against(center_low[5, group], w_query[...])
            + wide_b[rows:, :]
            + pad_rows(center_sum)
        )
        unit = center_wide[0, group]
        row_sums[0] += sum_pairs(grad_norm * unit)
        row_sums[3] += sum_pairs(grad_norm)
        yield
        result = middle_keep[group] + norm_back(
            unit, center_scale[0, group][:, :1], grad_norm * gain_center
        )
        target[group] = low(pad_rows(result[:TILE]))

    def edge_back(group, place, grad_gate, grad_edge, center_pair, sums):
        gain_sum, bias_sum = sums
        grad_norm = wide_b[place, :] + grad_gate * center_pair[: grad_gate.shape[0]]
        scale = three(scale_keep[group, place, :])
        unit = (
            wide(layer_in[group, place, :]) - three(mean_keep[group, place, :]) * inside
        ) * scale
        sums = (gain_sum + fold(grad_norm * unit), bias_sum + fold(grad_norm))
        return grad_edge + norm_back(unit, scale, grad_norm * gain_edge), sums

    def put_block(blocks, group, hidden, parts):
        rest = jnp.zeros((TILE, z.hidden_lanes - 3 * lanes), F32)
        below = [wide(center_low[k, group])[:TILE] for k in parts] + [rest]
        mine = group * z.gathers + (peers.first(last) if z.within else 0)
        blocks[mine] = low(
            jnp.concatenate([wide(hidden_low[hidden, group])[:TILE], jnp.concatenate(below, 1)], 0)
        )

    def left_gather(group):
        return Gather(peers, left_blocks, group, left_sems)

    def right_gather(group):
        return Gather(peers, right_blocks, group, right_sems)

    def push(gather, at):
        if not z.within:
            return
        for behind in range(last + 1):

            @pl.when(at >= behind)
            def _(behind=behind):
                gather(at - behind).push(last - behind)

    def push_rest(gather, behind):
        if not z.within:
            return
        for group in range(groups):
            stage = last - behind - (groups - 1 - group)
            if stage >= 0:
                gather(group).push(stage)

    def push_left(group):
        put_block(left_blocks, group, 0, (0, 1, 2))
        push(left_gather, group)

    def push_right(group):
        put_block(right_blocks, group, 1, (5, 4, 3))
        push(right_gather, group)

    def pack(target, matrix, extra=None):
        target[...] = jnp.where(lane < width, matrix[: z.sum_rows], 0.0)
        staging[: z.sum_part, :lanes] = matrix[z.sum_rows : z.sum_rows + z.sum_part]
        if extra is not None:
            staging[z.extra_at : z.extra_at + 6, :lanes] = extra
        rest = jnp.where(lane < width, staging[: z.sum_part, :lanes], 0.0)
        for part in range(z.sum_parts):
            place = slice(part * z.sum_part, (part + 1) * z.sum_part)
            target[place, :] += jnp.where(lane >= width, pltpu.roll(rest, z.shift(part), 1), 0.0)

    def fill_value():
        pack(value_sum, outer_sum(flat(context_keep[...]), flat(value_keep[...])))

    def fill_key():
        pack(key_sum, outer_sum(flat(score_keep[...]), flat(query_keep[...])) * scaling)

    def fill_edge():
        pack(edge_sum, edge_weight_sum[...], jnp.sum(row_sums[...], axis=1))

    if z.within:
        reductions = {
            "key": Reduction(near, key_sum, key_low, *key_pass, key_sems),
            "value": Reduction(near, value_sum, value_low, *value_pass, value_sems),
            "edge": LateReduction(near, edge_sum, edge_low, *edge_pass, edge_sems),
        }

    def advance(name, number):
        if z.within and number < reductions[name].steps:
            reductions[name].step(number)

    def side_copies(group):
        count = z.gathers * TILE
        place = pl.ds(group * count, count)
        return [
            pltpu.make_async_copy(kept.at[place], side.at[place], side_sem.at[index, group])
            for index, (kept, side) in enumerate(
                ((left_keep, left_side), (right_keep, right_side))
            )
        ]

    def final_copy(group):
        return pltpu.make_async_copy(final.at[group], final_result.at[group], final_sem.at[group])

    def sort_pair(at, first_left, second_left, first_right, second_right):
        place = pl.ds(pl.multiple_of(at * TILE, PAIR), PAIR)
        for first, second, kept in (
            (first_left, second_left, left_keep),
            (first_right, second_right, right_keep),
        ):
            first, second = wide(first), wide(second)
            kept[place, : z.hidden_lanes] = low(jnp.concatenate([first[:TILE], second[:TILE]], 0))
            kept[place, z.hidden_lanes :] = low(
                jnp.concatenate([first[TILE:], second[TILE:]], 0)
            )[:, : 3 * lanes]

    def sort_sides(group):
        left_gather(group).finish(0)
        right_gather(group).finish(0)
        first_block = group * z.gathers

        def one(at, carry):
            at = first_block + 2 * at
            sort_pair(at, *[side[at + k] for side in (left_blocks, right_blocks) for k in (0, 1)])
            return carry

        lax.fori_loop(0, z.gathers // 2, one, 0)
        for copy in side_copies(group):
            copy.start()

    def run(*steps, between=()):
        between = list(between)
        for step in steps:
            for _ in step:
                if between:
                    between.pop(0)()
        for work in between:
            work()

    def send(group, at):
        for copy in piece_copies(group, at):
            copy.start()

    def receive(group, at):
        for copy in piece_copies(group, at):
            copy.wait_recv()

    def gate_span(group, place, edge_norm, center_pair):
        gated[group, place, :] = low(edge_norm * center_pair[: edge_norm.shape[0]])

    def update_piece(group, at, sums):
        wide_a[:piece, :] = product(gated[group, whole_span(at), :], w_edge[...])
        results = []
        for place, changed in zip(spans(at), cut_blocks(wide_a[:piece, :])):
            result, sums = update_span(
                group, place, changed, wide(layer_in[group, place, :]), sums
            )
            results.append(result)
        return results, sums

    def weigh(group, at):
        edge_weight_sum[...] += outer_sum(
            gated[group, whole_span(at), :], live_grad[group, whole_span(at), :]
        )

    @pl.when(me == 0)
    def first_layer():
        unpack_center(layer_center)
        find_live()
        prepare_first()
        unpack_own(layer_in)
        norm_result[...] = jnp.zeros(norm_result.shape, F32)
        pl.semaphore_wait(barrier, len(neighbours))

        def forward_edges(group):
            center_pair = repeated(wide(norm_center(group)))

            def one(at, sums):
                open_piece(group, at)
                for place in spans(at):
                    edge_norm = norm_span(group, place, wide(layer_in[group, place, :]))
                    gate_span(group, place, edge_norm, center_pair)
                results, sums = update_piece(group, at, sums)
                put_blocks(group, at, results)
                at_once = (at < PIECES - 1) & ((group == 0) & (core == 0) if turns else True)
                pl.when(at_once)(lambda: send(group, at))
                return sums

            put_edge_norms(group, lax.fori_loop(0, PIECES, one, (zero_tile, zero_tile)))

        def forward_rest(group):
            @pl.when(group == 0)
            def _():
                prepare_rest()
                if turns:
                    pl.when(core == 0)(lambda: pass_turn(0))

            ask_center(group)
            run(forward_center(group), feed_center(group, sent_center))
            push_left(group)

        def send_rest(group):
            center_copy(group).start()
            send(group, PIECES - 1)

        def take_turn(group):
            pl.semaphore_wait(turn_sem, 1)
            for at in range(PIECES - 1):
                send(group, at)

        def pass_turn(group):
            for at in range(FIRST_PIECES):
                for copy in piece_copies(group, at):
                    copy.wait_send()
            pl.semaphore_signal(
                turn_sem, inc=1, device_id=peers.other(0, 1)[1], device_id_type=MESH_ID
            )

        def forward(step, carry):
            group = step // 2
            pl.when(step % 2 == 0)(lambda: forward_edges(group))
            pl.when(step % 2 == 1)(lambda: forward_rest(group))

            def hook(at, which, *works):
                @pl.when((step == at) & (core == which))
                def _():
                    for work, group in works:
                        work(group)

            if turns:
                hook(1, 0, (send_rest, 0))
                hook(1, 1, (take_turn, 0), (send_rest, 0))
                hook(2, 0, (take_turn, 1))
                hook(2, 1, (pass_turn, 0))
                hook(3, 0, (send_rest, 1), (pass_turn, 1))
                hook(4, 1, (take_turn, 1), (send_rest, 1))
                hook(5, 0, (take_turn, 2), (send_rest, 2))
                hook(5, 1, (pass_turn, 1))
            else:
                pl.when(step % 2 == 1)(lambda: send_rest(group))
            return carry

        lax.fori_loop(0, 2 * groups, forward, 0)
        push_rest(left_gather, 1)

        def backward(group, carry):
            center_copy(group).wait_recv()
            run(backward_center(group, got_center[group]))
            is_last = group == groups - 1

            @pl.when(is_last)
            def _():
                fill_value()
                advance("value", 0)

            run(score_center(group))
            push_right(group)
            if turns:
                pl.when((group == 0) & (core == 0))(lambda: pass_turn(2))

                @pl.when((group == 0) & (core == 1))
                def _():
                    take_turn(2)
                    send_rest(2)


            @pl.when(is_last)
            def _():
                fill_key()
                advance("key", 0)

            @pl.when(group == 0)
            def _():
                for behind in range(2, last + 1):
                    push_rest(left_gather, behind)

            center_pair = repeated(wide(center_low[0, group]))

            def one(at, carry):
                center_sum, sums = carry
                for number in range(PIECES):

                    @pl.when(is_last & (at == number))
                    def _(number=number):
                        if number == 2:
                            if last > 0:
                                push_rest(right_gather, 1)
                        else:
                            names = ("value", "key", "", "value", "key")
                            advance(names[number], number // 3 + 1)

                receive(group, at)
                for place, grad, (start, count) in zip(spans(at), get_blocks(group, at), blocks):
                    wide_c[start : start + count, :] = grad
                    live_grad[group, place, :] = low(grad * three(live_rows[group, place, :]))
                wide_a[:piece, :] = against(live_grad[group, whole_span(at), :], w_edge[...])
                for place, grad_gate, grad in zip(
                    spans(at), cut_blocks(wide_a[:piece, :]), cut_blocks(wide_c[:piece, :])
                ):
                    grad_gate = wide(low(grad_gate))
                    center_sum = center_sum + fold(grad_gate * wide(normed[group, place, :]))
                    result, sums = edge_back(group, place, grad_gate, grad, center_pair, sums)
                    final[group, place, :] = low(result)
                weigh(group, at)
                return center_sum, sums

            center_sum, sums = lax.fori_loop(
                0, PIECES, one, (zero_tile, (zero_tile, zero_tile))
            )
            gain_sum, bias_sum = sums
            row_sums[1] += gain_sum
            row_sums[4] += bias_sum
            run(finish_center(group, center_sum, center_result))
            final_copy(group).start()
            return carry

        lax.fori_loop(0, groups, backward, 0)

    @pl.when(me == 1)
    def second_layer():
        unpack_center(sent_center)
        find_live()
        norm_result[...] = jnp.zeros(norm_result.shape, F32)
        prepare_first()
        unpack_own(cotangent)
        prepare_rest()
        pl.semaphore_wait(barrier, len(neighbours))

        def gate(at, carry):
            group = at // PIECES
            at = at % PIECES
            open_piece(group, at)
            for place in spans(at):
                live_grad[group, place, :] = low(
                    wide(cotangent[group, place, :]) * three(live_rows[group, place, :])
                )
            gate_grad[group, whole_span(at), :] = low(
                against(live_grad[group, whole_span(at), :], w_edge[...])
            )
            return carry

        lax.fori_loop(0, groups * PIECES, gate, 0)

        def get_center(group):
            center_copy(group).wait_recv()
            layer_center[group] = got_center[group]
            norm_center(group)
            ask_center(group)

        def both(group, carry):
            def arrive(at, center_sum):
                pl.when(at == PIECES - 1)(lambda: get_center(group))
                receive(group, at)
                for place, values in zip(spans(at), get_blocks(group, at)):
                    layer_in[group, place, :] = low(values)
                    edge_norm = norm_span(group, place, values)
                    center_sum = center_sum + fold(edge_norm * wide(gate_grad[group, place, :]))
                return center_sum

            center_sum = lax.fori_loop(0, PIECES, arrive, zero_tile)
            center_pair = repeated(wide(center_low[0, group]))
            def leave(at, sums):
                results = []
                for place in spans(at):
                    result, sums = edge_back(
                        group,
                        place,
                        wide(gate_grad[group, place, :]),
                        wide(cotangent[group, place, :]),
                        center_pair,
                        sums,
                    )
                    results.append(result)
                put_blocks(group, at, results)
                send(group, at)
                return sums

            run(forward_center(group), backward_center(group, sent_center[group]))
            run(score_center(group), finish_center(group, center_sum, sent_center))
            center_copy(group).start()
            gain_sum, bias_sum = lax.fori_loop(0, PIECES, leave, (zero_tile, zero_tile))
            row_sums[1] += gain_sum
            row_sums[4] += bias_sum
            run(feed_center(group, center_result))
            push_left(group)
            push_right(group)
            return carry

        def update(group, carry):
            center_pair = repeated(wide(center_low[0, group]))

            def one(at, sums):
                for place in spans(at):
                    gate_span(group, place, wide(normed[group, place, :]), center_pair)
                results, sums = update_piece(group, at, sums)
                for place, result in zip(spans(at), results):
                    final[group, place, :] = low(result)
                weigh(group, at)
                return sums

            put_edge_norms(group, lax.fori_loop(0, PIECES, one, (zero_tile, zero_tile)))
            final_copy(group).start()
            return carry

        lax.fori_loop(0, groups, both, 0)
        fill_value()
        advance("value", 0)
        fill_key()
        advance("key", 0)
        lax.fori_loop(0, groups, update, 0)

    fill_edge()
    if z.within:
        advance("edge", 0)

        @pl.when(me == 1)
        def _():
            advance("value", 1)
            advance("key", 1)
            if last > 0:
                push_rest(left_gather, 1)
                push_rest(right_gather, 1)
            advance("value", 2)
            advance("key", 2)

        advance("edge", 1)
        advance("value", 3)
        advance("key", 3)
        for behind in range(2, last + 1):
            pl.when(me == 1)(lambda behind=behind: push_rest(left_gather, behind))
            push_rest(right_gather, behind)
        sort_sides(0)
        advance("edge", 2)
        advance("value", 4)
        advance("key", 4)
        for pair in range(1, groups):
            sort_sides(pair)
        advance("edge", 3)
        for reduction in reductions.values():
            reduction.drain()
        for group in range(groups):
            left_gather(group).drain()
            right_gather(group).drain()
            for copy in side_copies(group):
                copy.wait()
    else:
        fill_value()
        fill_key()
        for total, total_low in (
            (key_sum, key_low), (value_sum, value_low), (edge_sum, edge_low)
        ):
            total_low[...] = low(total[...])
        for at in range(0, z.blocks, 2):
            after = min(at + 1, z.blocks - 1)
            keep = 1.0 if at + 1 < z.blocks else 0.0
            sort_pair(
                at,
                left_blocks[at],
                wide(left_blocks[after]) * keep,
                right_blocks[at],
                wide(right_blocks[after]) * keep,
            )
        pltpu.sync_copy(left_keep, left_side)
        pltpu.sync_copy(right_keep, right_side)
    for group in range(groups):
        final_copy(group).wait()

    def sent(group, carry):
        center_copy(group).wait_send()
        for at in range(PIECES):
            waits = [copy.wait_send for copy in piece_copies(group, at)]
            if turns and at < FIRST_PIECES:
                pl.when((me == 1) | ((group == groups - 1) & (core == 1)))(
                    lambda waits=waits: [wait() for wait in waits] and None
                )
            else:
                for wait in waits:
                    wait()
        return carry

    lax.fori_loop(0, groups, sent, 0)


def result_kernel(
    z,
    center_ref,
    final,
    left_side,
    right_side,
    key_low,
    value_low,
    edge_low,
    norm_ref,
    center_result,
    edge_result,
    grad_square,
    grad_out,
    grad_up,
    grad_down,
    grad_gains,
    grad_biases,
    grad_hidden,
    norm_result,
):
    lanes, width, hidden, block = z.lanes, z.width, z.hidden, z.block
    lead = z.hidden_lanes

    def assemble(at, carry):
        place = pl.ds(pl.multiple_of(at * PAIR, PAIR), PAIR)
        parts = [wide(final[group, place, :]) for group in range(z.groups)]
        edge_result[2 * at] = low(jnp.concatenate([part[:TILE] for part in parts], 0))[:, :width]
        edge_result[2 * at + 1] = low(jnp.concatenate([part[TILE:] for part in parts], 0))[
            :, :width
        ]
        return carry

    lax.fori_loop(0, z.slots // 2, assemble, 0, unroll=2)
    center_result[...] = low(
        jnp.concatenate([wide(center_ref[group])[:TILE] for group in range(z.groups)], 0)
    )[:, :width]
    def part(side, index):
        return side[:, lead + index * lanes : lead + (index + 1) * lanes]

    query = outer_sum(part(left_side, 0), part(right_side, 0))
    attend = outer_sum(part(left_side, 1), part(right_side, 1))
    grow = outer_sum(part(left_side, 2), right_side[:, :lead])
    shrink = outer_sum(part(right_side, 2), left_side[:, :lead])
    lane = lax.broadcasted_iota(jnp.int32, (1, lanes), 1)

    def unpack(packed):
        rest = jnp.zeros((z.sum_part, lanes), F32)
        for index in range(z.sum_parts):
            held = wide(packed[index * z.sum_part : (index + 1) * z.sum_part, :])
            held = jnp.where(lane >= width, held, 0.0)
            rest = rest + pltpu.roll(held, (lanes - z.shift(index)) % lanes, 1)
        return jnp.concatenate([wide(packed[...]), rest], 0)

    key, value, edge = unpack(key_low), unpack(value_low), unpack(edge_low)
    sums = edge[block:]
    grad_square[:, 0, :] = query[:width, :width]
    grad_square[:, 1, :] = key[:width, :width]
    grad_square[:, 2, :] = value[:width, :width]
    grad_square[:, 3, :] = edge[:width, :width]
    grad_out[:, 0, :] = attend[:width, :width]
    grad_up[:, 0, :] = grow[:width, :hidden]
    grad_down[:, 0, :] = shrink[:width, :hidden]
    grad_gains[:, 0, :] = sums[0:3, :width]
    grad_biases[0:3, :] = sums[3:6, :width]
    for index, source in ((3, query), (4, value), (5, attend), (6, edge)):
        grad_biases[index : index + 1, :] = source[width : width + 1, :width]
    grad_biases[7:8, :] = jnp.sum(
        wide(part(right_side, 2)), axis=0, keepdims=True
    )[:, :width]
    grad_hidden[...] = grow[width : width + 1, :hidden]
    turned = jnp.concatenate([norm_ref[group] for group in range(z.groups)], 0).T
    norm_result[:, 0, :] = turned[:5]


def on_device(
    center_data,
    edge_data,
    leaf_counts,
    leaf_mask,
    square_weights,
    out_weight,
    up_weight,
    down_weight,
    norm_gains,
    biases,
    hidden_bias,
):
    star_count, model_width = center_data.shape[1:]
    slot_count = edge_data.shape[2]
    hidden_width = up_weight.shape[2]
    z = Sizes(star_count, slot_count, model_width, hidden_width, lax.axis_size("dp"))
    lanes, groups, rows = z.lanes, z.groups, z.rows
    heads = TILE * HEAD_ROWS
    stages = max(len(z.radices), 1)
    most = max(z.radices + [2])
    vmem = pltpu.VMEM
    shape = jax.ShapeDtypeStruct
    dma = pltpu.SemaphoreType.DMA

    def scatter_scratch(total, radices):
        sizes = scattered(total, radices)
        return (
            [vmem((size, lanes), BF16) for size in sizes],
            [vmem((r - 1, size // r, lanes), BF16) for size, r in zip(sizes, radices)],
        )

    near = flattened(z.radices)
    chips = near[1] if len(near) > 1 else 1
    sum_pass = scatter_scratch(z.sum_rows, near)
    sum_sems = [dma((max(len(near), 1), max(near + [2]) - 1))] * 4
    far, close = pl.BlockSpec(memory_space=pltpu.HBM), pl.BlockSpec(memory_space=vmem)
    between = pl.pallas_call(
        functools.partial(layer_kernel, z),
        out_shape=(
            shape((groups, PAIR, lanes), BF16),
            shape((groups, rows, lanes), BF16),
            shape((z.side_rows, z.factor_lanes), BF16),
            shape((z.side_rows, z.factor_lanes), BF16),
            shape((z.sum_rows, lanes), BF16),
            shape((z.sum_rows, lanes), BF16),
            shape((z.sum_rows, lanes), BF16),
            shape((groups, TILE, 128), F32),
        ),
        in_specs=[
            pl.BlockSpec(memory_space=pltpu.SMEM)
            if index == 2
            else far
            if index in (1, 4, 5, 6, 7)
            else close
            for index in range(11)
        ],
        out_specs=[far if index in (1, 2, 3) else close for index in range(8)],
        scratch_shapes=[
            vmem((groups, rows, lanes), BF16),
            vmem((z.side_rows, z.factor_lanes), BF16),
            vmem((z.side_rows, z.factor_lanes), BF16),
            vmem((groups, rows, lanes), BF16),
            vmem((groups, rows, lanes), BF16),
            vmem((groups, rows, z.main), BF16),
            vmem((groups, PIECES * z.tall, 128), BF16),
            vmem((groups, rows, z.main), BF16),
            vmem((groups, PIECES * z.tall, 128), BF16),
            vmem((groups, PAIR, lanes), BF16),
            vmem((groups, PAIR, lanes), BF16),
            vmem((groups, PAIR, lanes), BF16),
            vmem((groups, rows + PAIR, lanes), BF16),
            vmem((groups, rows, lanes), BF16),
            vmem((groups, rows, lanes), BF16),
            vmem((groups, rows, lanes), BF16),
            vmem((groups, rows, 128), F32),
            vmem((groups, rows, 128), F32),
            vmem((groups, rows, 128), F32),
            vmem((groups, PIECES, -(-z.slots // PIECES // TILE) * TILE, 128), F32),
            vmem((groups, rows + PAIR, 128), F32),
            vmem((groups, rows + PAIR, 128), F32),
            vmem((groups, rows + PAIR, 128), BF16),
            vmem((rows, lanes), F32),
            vmem((rows + PAIR, lanes), F32),
            vmem((rows, lanes), F32),
            vmem((max(z.sum_part, z.stars), z.hidden_lanes), F32),
            [vmem((4 * model_width, 128), F32)] * (lanes // 128),
            vmem((rows + PAIR, 128), BF16),
            vmem((lanes, lanes), BF16),
            vmem((lanes, lanes), BF16),
            vmem((lanes, lanes), BF16),
            vmem((lanes, lanes), BF16),
            vmem((lanes, lanes), BF16),
            vmem((lanes, z.hidden_lanes), BF16),
            vmem((lanes, z.hidden_lanes), BF16),
            vmem((TILE, lanes), F32),
            vmem((groups, heads, lanes), BF16),
            vmem((groups, heads, lanes), BF16),
            vmem((groups, heads, lanes), BF16),
            vmem((groups, heads, lanes), BF16),
            vmem((groups, heads, lanes), BF16),
            vmem((6, groups, PAIR, lanes), BF16),
            vmem((2, groups, PAIR, lanes), F32),
            vmem((2, groups, PAIR, 128), F32),
            vmem((2, groups, PAIR, z.hidden_lanes), BF16),
            vmem((groups, PAIR, z.hidden_lanes), F32),
            vmem((groups, PAIR, lanes), F32),
            vmem((groups, PAIR, lanes), F32),
            vmem((6, TILE, lanes), F32),
            vmem((lanes, lanes), F32),
            vmem((z.blocks, PAIR, z.hidden_lanes), BF16),
            vmem((z.blocks, PAIR, z.hidden_lanes), BF16),
            vmem((z.sum_rows, lanes), F32),
            vmem((z.sum_rows, lanes), F32),
            vmem((z.sum_rows, lanes), F32),
            sum_pass,
            sum_pass,
            [
                vmem((z.sum_rows, lanes), BF16),
                vmem((z.sum_rows, lanes), BF16),
                vmem((z.sum_rows, lanes), BF16),
                vmem((max(chips - 1, 1), z.sum_rows // chips, lanes), BF16),
            ],
            dma((groups, PIECES, 2)),
            dma((groups, PIECES, 2)),
            dma((2, groups)),
            dma((2, groups, stages, most - 1)),
            dma((2, groups, stages, most - 1)),
            sum_sems,
            sum_sems,
            sum_sems * 2,
            dma((2, groups)),
            dma((groups,)),
            pltpu.SemaphoreType.REGULAR,
            vmem((slot_count, star_count, model_width), BF16),
            vmem((model_width, 4, model_width), BF16),
            vmem((model_width, model_width), BF16),
            vmem((model_width, hidden_width), BF16),
            vmem((model_width, hidden_width), BF16),
            dma((4 + LOADS,)),
        ],
        compiler_params=pltpu.CompilerParams(
            collective_id=0, has_side_effects=True, vmem_limit_bytes=60 * 1024 * 1024
        ),
    )(
        center_data[0],
        jnp.transpose(edge_data[0], (1, 0, 2)),
        leaf_counts,
        leaf_mask,
        jnp.transpose(square_weights[0], (1, 0, 2)),
        out_weight[0],
        up_weight[0],
        down_weight[0].T,
        norm_gains[0],
        biases[0],
        hidden_bias,
    )
    outputs = pl.pallas_call(
        functools.partial(result_kernel, z),
        out_shape=(
            shape((star_count, model_width), BF16),
            shape((slot_count, star_count, model_width), BF16),
            shape((model_width, 4, model_width), F32),
            shape((model_width, 1, model_width), F32),
            shape((model_width, 1, hidden_width), F32),
            shape((model_width, 1, hidden_width), F32),
            shape((3, 1, model_width), F32),
            shape((8, model_width), F32),
            shape((1, hidden_width), F32),
            shape((5, 1, star_count), F32),
        ),
        in_specs=[pl.BlockSpec(memory_space=vmem)] * 8,
        out_specs=[pl.BlockSpec(memory_space=vmem)] * 10,
        compiler_params=pltpu.CompilerParams(vmem_limit_bytes=60 * 1024 * 1024),
    )(*between)
    center_result, edge_result, *sums, norm_rows = outputs
    if not z.within:
        sums = lax.psum(sums, "dp")
    square_sum, out_sum, up_sum, down_sum, gain_sum, bias_sum, hidden_sum = sums
    return (
        center_result[None],
        jnp.transpose(edge_result, (1, 0, 2))[None],
        jnp.transpose(square_sum, (1, 0, 2))[None],
        jnp.transpose(out_sum, (1, 0, 2)),
        jnp.transpose(up_sum, (1, 0, 2)),
        jnp.transpose(down_sum, (1, 2, 0)),
        jnp.transpose(gain_sum, (1, 0, 2)),
        bias_sum[None],
        hidden_sum,
        jnp.transpose(norm_rows, (1, 0, 2)),
    )


def solution(mesh):
    return jax.shard_map(
        on_device,
        mesh=mesh,
        in_specs=(
            P("section", "dp", None),
            P("section", "dp", None, None),
            P("dp"),
            P("dp", None),
            P("section", None, None, None),
            P("section", None, None),
            P("section", None, None),
            P("section", None, None),
            P("section", None, None),
            P("section", None, None),
            P("section", None),
        ),
        out_specs=(
            P("section", "dp", None),
            P("section", "dp", None, None),
            P("section", None, None, None),
            P("section", None, None),
            P("section", None, None),
            P("section", None, None),
            P("section", None, None),
            P("section", None, None),
            P("section", None),
            P("section", None, "dp"),
        ),
        check_vma=False,
    )
```

time: 1140 us -> 86.2 us (0.08); the launches traced: 1120 us -> 85.9 us
  matrix products: 354 us -> 0 us
  local copies, waits for them, and re-layouts: 344 us -> 0 us
  other arithmetic: 226 us -> 0 us
  Pallas kernels: 0 us -> 85.1 us
  blocking collectives: 62.6 us -> 0 us
  waiting for transfers between devices: 60 us -> 0 us
  starting transfers between devices: 49 us -> 0 us
  between operations: 21 us -> 0.81 us
    dot_general x273 -> x0, matrix products: 354 us -> none  [the longest x105 122 us: product(): return jnp.dot(operand, factor, preferred_element_type=jnp.float32)]
    reshape x117 -> x0, local copies, waits for them, and re-layouts: 127 us -> none  [the longest x21 21.7 us: forward_layer(): query_heads = query.reshape(star_count, HEADS, head_size)]
    reduce_sum x140 -> x0, other arithmetic: 97.3 us -> none  [the longest x40 32.8 us: total_rows(): return jnp.sum(values.astype(jnp.float32), axis=0)]
    pallas_call x0 -> x2, Pallas kernels: none -> 85.1 us  [the longest x1 77.8 us: on_device(): pl.pallas_call(functools.partial(layer_kernel, z), out_shape=(shape((grou...]
    psum x1 -> x0, blocking collectives: 62.6 us -> none  [on_device(): lax.psum((partial_value[0], partial_value[1], partial_value[2], partial_v...]
    psum x1 -> x0, waiting for transfers between devices: 59.9 us -> none  [on_device(): lax.psum((partial_value[0], partial_value[1], partial_value[2], partial_v...]
    dot_general x44 -> x0, local copies, waits for them, and re-layouts: 53.2 us -> none  [the longest x30 48.9 us: product(): return jnp.dot(operand, factor, preferred_element_type=jnp.float32)]
    ppermute x24 -> x0, starting transfers between devices: 49 us -> none  [passed_along(): return lax.ppermute(block, axis, route)]
  transfers between devices with their start and end apart: 25 -> 0, of which waited for: 1 -> 0; matrix products, arithmetic and copies ran while one was open for 54% -> 0% of each run, Pallas kernels for 0% -> 0%
where the time goes in v1:
time: 86.2 us; the launch traced here: 85.9 us
  Pallas kernels  85.1 us (99%)
    pallas_call x1, Pallas kernels, on_device(): pl.pallas_call(functools.partial(layer_kernel, z), out_shape=(shape((grou...  77.8 us
    pallas_call x1, Pallas kernels, on_device(): pl.pallas_call(functools.partial(result_kernel, z), out_shape=(shape((sta...  7.3 us

profile of v1, /device:TPU:0, one launch (start us, length us, event | category | flops | bytes accessed | tf_op | source)
XLA Modules:
  0.0 85.9 jit_solution(14715333835749190005)
XLA Ops:
  0.6 77.8 %shard_map.186 = (bf16[3,16,384]{2,1,0:T(8,128)(2,1)}, bf16[3,800,384]{2,1,0:T(8,128)(2,1)}, bf16[384,2432]{1,0:T(8,128)(2,1)}, bf16[384,2432]{1,0:T(8,128)(2,1)...) custom-call(bf16[24,300]{1,0:T(8,128)(2,1)} %bitcast.32, ...), custom_call_target="tpu_custom_call" | custom-call | tf_op jit(solution)/shard_map/pallas_call | solution.py:1466
  78.5 7.3 %shard_map.187 = (bf16[24,300]{1,0:T(8,128)(2,1)}, bf16[100,24,300]{2,1,0:T(8,128)(2,1)}, f32[300,4,300]{2,1,0:T(4,128)}, f32[300,1,300]{2,1,0:T(1,128)}, f32[30...) custom-call(bf16[3,16,384]{2,1,0:T(8,128)(2,1)} %get-tuple-element.2, ...), custom_call_target="tpu_custom_call" | custom-call | tf_op jit(solution)/shard_map/pallas_call | solution.py:1586
